TPU v7x, 256 devices: a whole 4x4x8 slice. The times are simulated.
256 devices in a mesh: grp: 2 (over x_lo), seq: 16 (over y, x_hi, core), rep: 8 (over z).
Axes of the slice: x: 4 (x_hi: 2, x_lo: 2; x = x_hi * 2 + x_lo), y: 4, z: 8, core: 2. Of those that a mesh axis runs over, the one named last changes fastest.
Arguments:
- pre_query: bfloat16 [2, 4096, 8192], P('grp', 'seq', 'rep'), may hold values from -6 to 6
- history_key: bfloat16 [2, 2048, 1024], P('grp', 'seq', 'rep'), may hold values from -6 to 6
- history_value: bfloat16 [2, 2048, 1024], P('grp', 'seq', 'rep'), may hold values from -6 to 6
- document_key: bfloat16 [2, 4096, 1024], P('grp', 'seq', 'rep'), may hold values from -6 to 6
- document_value: bfloat16 [2, 4096, 1024], P('grp', 'seq', 'rep'), may hold values from -6 to 6
- stretch_start: int32 [2], P('grp'), may hold values from 1024 to 2048
- decode_query: bfloat16 [512, 4, 8192], P(('grp', 'rep'), None, 'seq'), may hold values from -6 to 6
- cached_row_keys: bfloat16 [512, 16, 256, 128], P(('grp', 'rep'), 'seq'), may hold values from -6 to 6
- cached_row_values: bfloat16 [512, 16, 256, 128], P(('grp', 'rep'), 'seq'), may hold values from -6 to 6
- cache_lengths: int32 [512], P(('grp', 'rep')), may hold values from 1 to 512, as said below
- doc_owner: int32 [512], P(('grp', 'rep')), may hold values from 0 to 1
- decode_key: bfloat16 [512, 4, 1024], P(('grp', 'rep')), may hold values from -6 to 6
- decode_value: bfloat16 [512, 4, 1024], P(('grp', 'rep')), may hold values from -6 to 6
Outputs:
- prefill_output: bfloat16 [2, 4096, 8192], P('grp', 'seq', 'rep')
- dec_out: bfloat16 [512, 4, 8192], P(('grp', 'rep'), None, 'seq')
Inputs may be any that keep to these rules, and one draw needn't show every extreme that they name: `cache_lengths`: some row has exactly 512 valid positions.
All inputs are finite; a program needn't handle non-finite values.
Results may differ from a plain program's by a relative error of at most 0.019.
Values may be sent and summed in bfloat16 or wider, within the bound.
A program may use at most 128 MiB of HBM per device.

v0:
```python
import jax
import jax.numpy as jnp
from jax import lax
from jax.sharding import PartitionSpec as P

KEY_VALUE_HEADS = 8
HEAD_SIZE = 128
GROUP_QUERIES = 8


def partner(x, axis, stride):
    return lax.ppermute(x, axis, [(i, i ^ 1 << stride) for i in range(lax.axis_size(axis))])


def online_update(state, scores, visible, value_rows, form):
    top, total, summed = state
    masked = jnp.where(visible, scores, jnp.float32(-1e30))
    new_top = jnp.maximum(top, jnp.max(masked, axis=-1))
    factor = jnp.exp(top - new_top)
    weights = jnp.where(visible, jnp.exp(scores - new_top[..., None]), jnp.float32(0.0))
    total = total * factor + jnp.sum(weights, axis=-1)
    summed = summed * factor[..., None] + jnp.einsum(
        form, weights.astype(jnp.bfloat16), value_rows, preferred_element_type=jnp.float32
    )
    return (new_top, total, summed)


def combine_parts(first, second):
    top = jnp.maximum(first[0], second[0])
    left = jnp.exp(first[0] - top)
    right = jnp.exp(second[0] - top)
    return (
        top,
        first[1] * left + second[1] * right,
        first[2] * left[..., None] + second[2] * right[..., None],
    )


def local(
    pre_query,
    history_key,
    history_value,
    document_key,
    document_value,
    stretch_start,
    decode_query,
    cached_row_keys,
    cached_row_values,
    cache_lengths,
    doc_owner,
    decode_key,
    decode_value,
):
    scale = HEAD_SIZE ** (-0.5)
    seq_index = lax.axis_index("seq")
    grp_index = lax.axis_index("grp")
    queries = pre_query[0]
    stretch_rows = queries.shape[0]
    hist_rows = history_key.shape[1]
    kv_local = history_key.shape[2] // HEAD_SIZE
    span = hist_rows + stretch_rows
    query_pos = seq_index * stretch_rows + jnp.arange(stretch_rows, dtype=jnp.int32)
    start_slot = stretch_start[0]
    keys_joined = jnp.concatenate([history_key[0], document_key[0]], axis=0)
    values_joined = jnp.concatenate([history_value[0], document_value[0]], axis=0)
    query_four = queries.reshape(stretch_rows, kv_local, GROUP_QUERIES, HEAD_SIZE)
    start_state = (
        jnp.full((stretch_rows, kv_local, GROUP_QUERIES), -1e30, jnp.float32),
        jnp.zeros((stretch_rows, kv_local, GROUP_QUERIES), jnp.float32),
        jnp.zeros((stretch_rows, kv_local, GROUP_QUERIES, HEAD_SIZE), jnp.float32),
    )
    piece_keys = lax.all_gather(keys_joined, "seq", axis=0, tiled=True)
    piece_values = lax.all_gather(values_joined, "seq", axis=0, tiled=True)
    count = piece_keys.shape[0]
    width = 512

    def one_block(state, offset):
        key_rows = lax.dynamic_slice_in_dim(piece_keys, offset, width, 0).reshape(
            width, kv_local, HEAD_SIZE
        )
        value_rows = lax.dynamic_slice_in_dim(piece_values, offset, width, 0).reshape(
            width, kv_local, HEAD_SIZE
        )
        slot = offset + jnp.arange(width, dtype=jnp.int32)
        shard = slot // span
        within = slot % span
        hist_ok = shard * hist_rows + within < start_slot
        stretch_ok = (shard * stretch_rows + within - hist_rows)[None, :] <= query_pos[:, None]
        visible = jnp.where((within < hist_rows)[None, :], hist_ok[None, :], stretch_ok)
        scores = (
            jnp.einsum("ihgd,khd->ihgk", query_four, key_rows, preferred_element_type=jnp.float32)
            * scale
        )
        return (
            online_update(state, scores, visible[:, None, None, :], value_rows, "ihgk,khd->ihgd"),
            None,
        )

    offsets = jnp.arange(count // width, dtype=jnp.int32) * width
    top, total, summed = lax.scan(one_block, start_state, offsets)[0]
    prefill_output = (
        (summed / total[..., None])
        .astype(jnp.bfloat16)
        .reshape(1, stretch_rows, kv_local * GROUP_QUERIES * HEAD_SIZE)
    )
    sequence_size = lax.axis_size("seq")
    stored_entries = cached_row_keys.shape[1]
    split_count = stored_entries * sequence_size // KEY_VALUE_HEADS
    level_list = split_count.bit_length() - 1
    run = seq_index % split_count
    base_head = seq_index * stored_entries // split_count
    rows_dev = decode_query.shape[0]
    steps = decode_query.shape[1]
    own_heads = decode_query.shape[2] // HEAD_SIZE
    rows_per_run = stretch_rows // split_count
    first_group = grp_index == 0
    gathered_query = decode_query.reshape(rows_dev, steps, own_heads, HEAD_SIZE)
    level = 0
    other_query = partner(gathered_query, "seq", level)
    lower = run // 2**level % 2 == 0
    gathered_query = jnp.where(
        lower,
        jnp.concatenate([gathered_query, other_query], axis=2),
        jnp.concatenate([other_query, gathered_query], axis=2),
    )
    query_five = gathered_query.reshape(rows_dev, steps, stored_entries, GROUP_QUERIES, HEAD_SIZE)
    state = (
        jnp.full((rows_dev, steps, stored_entries, GROUP_QUERIES), -1e30, jnp.float32),
        jnp.zeros((rows_dev, steps, stored_entries, GROUP_QUERIES), jnp.float32),
        jnp.zeros((rows_dev, steps, stored_entries, GROUP_QUERIES, HEAD_SIZE), jnp.float32),
    )
    complete_key, complete_value = (
        lax.all_gather(document_key[0], "rep", axis=1, tiled=True),
        lax.all_gather(document_value[0], "rep", axis=1, tiled=True),
    )
    run_key = (
        complete_key.reshape(split_count, rows_per_run, KEY_VALUE_HEADS, HEAD_SIZE)
        .transpose(1, 2, 0, 3)
        .reshape(rows_per_run, KEY_VALUE_HEADS * split_count, HEAD_SIZE)
    )
    run_value = (
        complete_value.reshape(split_count, rows_per_run, KEY_VALUE_HEADS, HEAD_SIZE)
        .transpose(1, 2, 0, 3)
        .reshape(rows_per_run, KEY_VALUE_HEADS * split_count, HEAD_SIZE)
    )
    own_key, own_value = (
        lax.all_to_all(run_key, "seq", split_axis=1, concat_axis=0, tiled=True),
        lax.all_to_all(run_value, "seq", split_axis=1, concat_axis=0, tiled=True),
    )
    far_key, far_value = partner((own_key, own_value), "grp", 0)
    doc_key = jnp.where(first_group, jnp.stack([own_key, far_key]), jnp.stack([far_key, own_key]))
    doc_value = jnp.where(
        first_group, jnp.stack([own_value, far_value]), jnp.stack([far_value, own_value])
    )
    current = state
    for owning_device in range(2):
        scores = (
            jnp.einsum(
                "rtcgd,ncd->rtcgn",
                query_five,
                doc_key[owning_device],
                preferred_element_type=jnp.float32,
            )
            * scale
        )
        visible = (doc_owner == owning_device)[:, None, None, None, None]
        current = online_update(
            current, scores, visible, doc_value[owning_device], "rtcgn,ncd->rtcgd"
        )
    state = current
    run_slots = cached_row_keys.shape[2]
    positions = run * run_slots + jnp.arange(run_slots, dtype=jnp.int32)
    cache_visible = (positions[None, :] < cache_lengths[:, None])[:, None, None, None, :]
    scores = (
        jnp.einsum(
            "rtcgd,rcpd->rtcgp", query_five, cached_row_keys, preferred_element_type=jnp.float32
        )
        * scale
    )
    state = online_update(state, scores, cache_visible, cached_row_values, "rtcgp,rcpd->rtcgd")
    new_key = lax.dynamic_slice_in_dim(
        decode_key, base_head * HEAD_SIZE, stored_entries * HEAD_SIZE, 2
    ).reshape(rows_dev, steps, stored_entries, HEAD_SIZE)
    new_value = lax.dynamic_slice_in_dim(
        decode_value, base_head * HEAD_SIZE, stored_entries * HEAD_SIZE, 2
    ).reshape(rows_dev, steps, stored_entries, HEAD_SIZE)
    step_ids = jnp.arange(steps, dtype=jnp.int32)
    new_visible = ((step_ids[None, :] <= step_ids[:, None]) & (run == 0))[None, :, None, None, :]
    scores = (
        jnp.einsum("rtcgd,rucd->rtcgu", query_five, new_key, preferred_element_type=jnp.float32)
        * scale
    )
    state = online_update(state, scores, new_visible, new_value, "rtcgu,rucd->rtcgd")
    flat_heads = stored_entries * GROUP_QUERIES
    state = (
        state[0].reshape(rows_dev, steps, flat_heads),
        state[1].reshape(rows_dev, steps, flat_heads),
        state[2].reshape(rows_dev, steps, flat_heads, HEAD_SIZE),
    )
    level = 0
    received = (
        partner(state[0].astype(jnp.bfloat16), "seq", level).astype(jnp.float32),
        partner(state[1].astype(jnp.bfloat16), "seq", level).astype(jnp.float32),
        partner(state[2].astype(jnp.bfloat16), "seq", level).astype(jnp.float32),
    )
    state = combine_parts(state, received)
    first_head = run * own_heads * (level_list > 0)
    total = lax.dynamic_slice_in_dim(state[1], first_head, own_heads, 2)
    summed = lax.dynamic_slice_in_dim(state[2], first_head, own_heads, 2)
    dec_out = (
        (summed / total[..., None])
        .astype(jnp.bfloat16)
        .reshape(rows_dev, steps, own_heads * HEAD_SIZE)
    )
    return (prefill_output, dec_out)


def solution(mesh):
    placed = (
        P("grp", "seq", "rep"),
        P("grp", "seq", "rep"),
        P("grp", "seq", "rep"),
        P("grp", "seq", "rep"),
        P("grp", "seq", "rep"),
        P("grp"),
        P(("grp", "rep"), None, "seq"),
        P(("grp", "rep"), "seq", None, None),
        P(("grp", "rep"), "seq", None, None),
        P(("grp", "rep")),
        P(("grp", "rep")),
        P(("grp", "rep"), None, None),
        P(("grp", "rep"), None, None),
    )
    return jax.shard_map(
        local,
        mesh=mesh,
        in_specs=placed,
        out_specs=(P("grp", "seq", "rep"), P(("grp", "rep"), None, "seq")),
        check_vma=False,
    )
```

profile of v0, /device:TPU:1, one launch (start us, length us, event | category | flops | bytes accessed | tf_op | source)
XLA Modules:
  0.0 319.7 jit_solution(3762336432974219428)
XLA Ops:
  10.9 3.3 %collective-permute-start.1 = (bf16[32,4,4,128]{3,2,1,0:T(4,128)(2,1)S(1)}, bf16[32,4,4,128]{3,2,1,0:T(4,128)(2,1)S(1)}, u32[]{:S(2)}, u32[]{:S(2)}) collective-permute-start(bf16[32,4,4,128]{3,2,1,0:T(4,128)(2,1)S(1)} %concatenate.58), channel_id=1, source_target_pairs={{0,8},{8,0},{16,24},{24,16},{32,40},{40,32},{48,56},{56,48},{64,72... | collective-permute-start | bytes 393224 | tf_op jit(solution)/shard_map/ppermute | solution.py:12
  14.2 21.7 %all-gather = bf16[1,256,1024]{2,1,0:T(8,128)(2,1)S(1)} all-gather(bf16[1,256,128]{2,1,0:T(8,128)(2,1)} %param.18), channel_id=2, replica_groups=mesh['grp'=2,'seq'=16,'rep'=8] {'rep'}, dimensions={2}, use_global_device_ids=true | all-gather | bytes 589824 | tf_op jit(solution)/shard_map/all_gather | solution.py:133
  36.9 11.6 %all-to-all-start = ((bf16[128,16,128]{2,0,1:T(8,128)(2,1)}), bf16[128,16,128]{2,0,1:T(8,128)(2,1)}, u32[]{:S(2)}, u32[]{:S(2)}) async-start(bf16[128,16,128]{2,0,1:T(8,128)(2,1)} %bitcast.9), calls=%async_computation | async-start | bytes 1048576 | tf_op jit(solution)/shard_map/all_to_all | solution.py:147
  49.3 19.9 %all-gather.1 = bf16[1,256,1024]{2,1,0:T(8,128)(2,1)S(1)} all-gather(bf16[1,256,128]{2,1,0:T(8,128)(2,1)S(1)} %copy-done.11), channel_id=3, replica_groups=mesh['grp'=2,'seq'=16,'rep'=8] {'rep'}, dimensions={2}, use_global_device_ids=true | all-gather | bytes 589824 | tf_op jit(solution)/shard_map/all_gather | solution.py:134
  70.3 10.9 %all-to-all-start.1 = ((bf16[128,16,128]{2,0,1:T(8,128)(2,1)}), bf16[128,16,128]{2,0,1:T(8,128)(2,1)}, u32[]{:S(2)}, u32[]{:S(2)}) async-start(bf16[128,16,128]{2,0,1:T(8,128)(2,1)} %bitcast.22), calls=%async_computation.1 | async-start | bytes 1048576 | tf_op jit(solution)/shard_map/all_to_all | solution.py:148
  82.9 3.4 %select_reduce_fusion.1 = (f32[32,4,8]{2,1,0:T(4,128)}, f32[32,4,1,8,4]{3,4,1,0,2:T(4,128)}) fusion(pred[4,4]{1,0:T(4,128)(4,1)S(1)} %fusion.120, bf16[32,4,8,128]{3,2,1,0:T(8,128)(2,1)S(1)} %maximum_select_fusion.2, bf16[32,4,1024]{2,1,0:T(4,128)(2,1)} %param.26, s32[]{:T(128)S(6)} %select_n.197), kind=kOutput, calls=%fused_computation.106 | convolution fusion | flops 1059840 | bytes 315412 | tf_op jit(solution)/shard_map/rtcgd,rucd->rtcgu/dot_general | solution.py:190
  87.2 6.1 %all-to-all-done.1 = bf16[128,16,128]{2,0,1:T(8,128)(2,1)} async-done(((bf16[128,16,128]{2,0,1:T(8,128)(2,1)}), bf16[128,16,128]{2,0,1:T(8,128)(2,1)}, u32[]{:S(2)}, u32[]{:S(2)}) %all-to-all-start.1) | async-done | bytes 524320 | tf_op jit(solution)/shard_map/all_to_all | solution.py:148
  93.3 7.8 %collective-permute-done = bf16[2048,1,128]{2,0,1:T(8,128)(2,1)} collective-permute-done((bf16[2048,1,128]{2,0,1:T(8,128)(2,1)}, bf16[2048,1,128]{2,0,1:T(8,128)(2,1)}, u32[]{:S(2)}, u32[]{:S(2)}) %collective-permute-start) | collective-permute-done | bytes 524320 | tf_op jit(solution)/shard_map/ppermute | solution.py:12
  101.1 1.7 maximum_select_fusion
  102.8 1.5 fusion.33
  104.4 1.5 fusion.36
  107.6 5.0 %bitcast_reduce_fusion = (f32[32,4,8]{0,2,1:T(8,128)}, f32[32,4,8]{0,2,1:T(8,128)}) fusion(f32[2048,32,4,8]{0,1,3,2:T(8,128)S(1)} %get-tuple-element.260, f32[32,4,8]{0,2,1:T(8,128)S(1)} %get-tuple-element.236, pred[32]{0:T(512)(128)(4,1)S(1)} %copy-done.20, f32[32,4,8]{0,2,1:T(8,128)S(1)} %get-tuple-element.252, ...), kind=kLoop, calls=%fused_computation.43 | loop fusion | flops 16775168 | bytes 16793664 | tf_op jit(solution)/shard_map/reduce_sum | solution.py:21
  113.5 1.9 fusion.106
  115.4 1.7 bitcast_reduce_fusion.2
  117.2 2.7 maximum_select_fusion.1
  119.9 2.0 fusion.47
  123.2 1.4 fusion.115
  124.7 5.1 %fusion.69 = f32[1,128,32,4,8]{1,2,4,3,0:T(8,128)S(1)} fusion(f32[2048,32,4,8]{0,1,3,2:T(8,128)} %copy-done.3, f32[32,4,8]{0,2,1:T(8,128)} %copy-done.17, pred[32]{0:T(512)(128)(4,1)} %copy-done.22, bf16[2,2048,1,128]{3,1,2,0:T(8,128)(2,1)} %maximum_select_fusion.1, f32[32,4,8]{0,2,1:T(8,128)S(1)} %get-tuple-element.250, f32[32,4,8]{0,2,1:T(8,128)S(1)} %get-tuple-element.251), kind=kOutput, calls=%fused_computation.73 | convolution fusion | flops 545521664 | bytes 9462272 | tf_op jit(solution)/shard_map/rtcgn,ncd->rtcgd/dot_general | solution.py:22
  129.9 6.8 %fusion.131 = (bf16[32,4,8,128]{3,0,2,1:T(8,128)(2,1)}, f32[32,4,8,128]{3,0,2,1:T(8,128)}) fusion(f32[32,128,4,8]{1,3,2,0:T(8,128)S(1)} %copy-done.9, f32[32,4,8]{0,2,1:T(8,128)S(1)} %get-tuple-element.248, f32[32,4,8,128]{3,2,1,0:T(8,128)S(1)} %copy-done.7, f32[32,4,8]{0,2,1:T(8,128)S(1)} %get-tuple-element.249, f32[1,128,32,4,8]{1,2,4,3,0:T(8,128)S(1)} %fusion.69, ...), kind=kOutput, calls=%fused_computation.155 | convolution fusion | flops 546045952 | bytes 11321856 | tf_op jit(solution)/shard_map/rtcgn,ncd->rtcgd/dot_general | solution.py:22
  140.5 170.1 %while.17 = (s32[]{:T(128)}, f32[256,1,8]{0,2,1:T(8,128)S(1)}, f32[256,1,8]{0,2,1:T(8,128)S(1)}, f32[256,1,8,128]{0,3,2,1:T(8,128)}, s32[12]{0:T(128)S(1)}, /*in...) while((s32[]{:T(128)}, f32[256,1,8]{0,2,1:T(8,128)S(1)}, ...), condition=%wide.region_3.4_spmd.clone, body=%wide.region_0.3_spmd.clone.sunk | while | flops 549483264 | bytes 32907496 | solution.py:100
  141.0 1.3 add_compare_fusion.2
  145.3 3.6 %fusion.142 = (f32[256,8]{0,1:T(8,128)S(1)}, f32[512,256,8]{1,0,2:T(8,128)}) fusion(pred[256,512]{0,1:T(8,128)(4,1)S(1)} %compare_select_fusion.2, bf16[256,1,8,128]{3,0,2,1:T(8,128)(2,1)S(1)} %get-tuple-element.373, bf16[6144,128]{1,0:T(8,128)(2,1)} %get-tuple-element.372, s32[]{:T(128)S(6)} %select_n.322), kind=kOutput, calls=%fused_computation.3.clone.1 | convolution fusion | flops 271579136 | bytes 4988932 | tf_op jit(solution)/shard_map/while/body/eval_jaxpr/ihgd,khd->ihgk/dot_general | solution.py:91
  148.9 4.5 %fusion.145 = f32[256,1,8,128]{0,3,2,1:T(8,128)} fusion(f32[512,256,8]{1,0,2:T(8,128)} %get-tuple-element.338, f32[256,8]{0,1:T(8,128)S(1)} %bitcast.375, pred[256,512]{0,1:T(8,128)(4,1)S(1)} %compare_select_fusion.2, f32[256,1,8,128]{0,3,2,1:T(8,128)} %get-tuple-element.356, f32[256,8]{0,1:T(8,128)S(1)} %get-tuple-element.339, pred[]{:T(512)S(6)} %compare.8, ...), kind=kOutput, calls=%fused_computation.12.clone.1 | convolution fusion | flops 273416192 | bytes 6569989 | tf_op jit(solution)/shard_map/while/body/eval_jaxpr/ihgk,khd->ihgd/dot_general | solution.py:22
  154.9 1.3 add_compare_fusion.2
  159.2 3.6 %fusion.142 = (f32[256,8]{0,1:T(8,128)S(1)}, f32[512,256,8]{1,0,2:T(8,128)}) fusion(pred[256,512]{0,1:T(8,128)(4,1)S(1)} %compare_select_fusion.2, bf16[256,1,8,128]{3,0,2,1:T(8,128)(2,1)S(1)} %get-tuple-element.373, bf16[6144,128]{1,0:T(8,128)(2,1)} %get-tuple-element.372, s32[]{:T(128)S(6)} %select_n.322), kind=kOutput, calls=%fused_computation.3.clone.1 | convolution fusion | flops 271579136 | bytes 4988932 | tf_op jit(solution)/shard_map/while/body/eval_jaxpr/ihgd,khd->ihgk/dot_general | solution.py:91
  162.8 4.8 %fusion.145 = f32[256,1,8,128]{0,3,2,1:T(8,128)} fusion(f32[512,256,8]{1,0,2:T(8,128)} %get-tuple-element.338, f32[256,8]{0,1:T(8,128)S(1)} %bitcast.375, pred[256,512]{0,1:T(8,128)(4,1)S(1)} %compare_select_fusion.2, f32[256,1,8,128]{0,3,2,1:T(8,128)} %get-tuple-element.356, f32[256,8]{0,1:T(8,128)S(1)} %get-tuple-element.339, pred[]{:T(512)S(6)} %compare.8, ...), kind=kOutput, calls=%fused_computation.12.clone.1 | convolution fusion | flops 273416192 | bytes 6569989 | tf_op jit(solution)/shard_map/while/body/eval_jaxpr/ihgk,khd->ihgd/dot_general | solution.py:22
  169.1 1.3 add_compare_fusion.2
  173.4 3.6 %fusion.142 = (f32[256,8]{0,1:T(8,128)S(1)}, f32[512,256,8]{1,0,2:T(8,128)}) fusion(pred[256,512]{0,1:T(8,128)(4,1)S(1)} %compare_select_fusion.2, bf16[256,1,8,128]{3,0,2,1:T(8,128)(2,1)S(1)} %get-tuple-element.373, bf16[6144,128]{1,0:T(8,128)(2,1)} %get-tuple-element.372, s32[]{:T(128)S(6)} %select_n.322), kind=kOutput, calls=%fused_computation.3.clone.1 | convolution fusion | flops 271579136 | bytes 4988932 | tf_op jit(solution)/shard_map/while/body/eval_jaxpr/ihgd,khd->ihgk/dot_general | solution.py:91
  177.0 4.8 %fusion.145 = f32[256,1,8,128]{0,3,2,1:T(8,128)} fusion(f32[512,256,8]{1,0,2:T(8,128)} %get-tuple-element.338, f32[256,8]{0,1:T(8,128)S(1)} %bitcast.375, pred[256,512]{0,1:T(8,128)(4,1)S(1)} %compare_select_fusion.2, f32[256,1,8,128]{0,3,2,1:T(8,128)} %get-tuple-element.356, f32[256,8]{0,1:T(8,128)S(1)} %get-tuple-element.339, pred[]{:T(512)S(6)} %compare.8, ...), kind=kOutput, calls=%fused_computation.12.clone.1 | convolution fusion | flops 273416192 | bytes 6569989 | tf_op jit(solution)/shard_map/while/body/eval_jaxpr/ihgk,khd->ihgd/dot_general | solution.py:22
  183.3 1.3 add_compare_fusion.2
  187.6 3.6 %fusion.142 = (f32[256,8]{0,1:T(8,128)S(1)}, f32[512,256,8]{1,0,2:T(8,128)}) fusion(pred[256,512]{0,1:T(8,128)(4,1)S(1)} %compare_select_fusion.2, bf16[256,1,8,128]{3,0,2,1:T(8,128)(2,1)S(1)} %get-tuple-element.373, bf16[6144,128]{1,0:T(8,128)(2,1)} %get-tuple-element.372, s32[]{:T(128)S(6)} %select_n.322), kind=kOutput, calls=%fused_computation.3.clone.1 | convolution fusion | flops 271579136 | bytes 4988932 | tf_op jit(solution)/shard_map/while/body/eval_jaxpr/ihgd,khd->ihgk/dot_general | solution.py:91
  191.2 4.8 %fusion.145 = f32[256,1,8,128]{0,3,2,1:T(8,128)} fusion(f32[512,256,8]{1,0,2:T(8,128)} %get-tuple-element.338, f32[256,8]{0,1:T(8,128)S(1)} %bitcast.375, pred[256,512]{0,1:T(8,128)(4,1)S(1)} %compare_select_fusion.2, f32[256,1,8,128]{0,3,2,1:T(8,128)} %get-tuple-element.356, f32[256,8]{0,1:T(8,128)S(1)} %get-tuple-element.339, pred[]{:T(512)S(6)} %compare.8, ...), kind=kOutput, calls=%fused_computation.12.clone.1 | convolution fusion | flops 273416192 | bytes 6569989 | tf_op jit(solution)/shard_map/while/body/eval_jaxpr/ihgk,khd->ihgd/dot_general | solution.py:22
  201.8 3.6 %fusion.142 = (f32[256,8]{0,1:T(8,128)S(1)}, f32[512,256,8]{1,0,2:T(8,128)}) fusion(pred[256,512]{0,1:T(8,128)(4,1)S(1)} %compare_select_fusion.2, bf16[256,1,8,128]{3,0,2,1:T(8,128)(2,1)S(1)} %get-tuple-element.373, bf16[6144,128]{1,0:T(8,128)(2,1)} %get-tuple-element.372, s32[]{:T(128)S(6)} %select_n.322), kind=kOutput, calls=%fused_computation.3.clone.1 | convolution fusion | flops 271579136 | bytes 4988932 | tf_op jit(solution)/shard_map/while/body/eval_jaxpr/ihgd,khd->ihgk/dot_general | solution.py:91
  205.4 4.8 %fusion.145 = f32[256,1,8,128]{0,3,2,1:T(8,128)} fusion(f32[512,256,8]{1,0,2:T(8,128)} %get-tuple-element.338, f32[256,8]{0,1:T(8,128)S(1)} %bitcast.375, pred[256,512]{0,1:T(8,128)(4,1)S(1)} %compare_select_fusion.2, f32[256,1,8,128]{0,3,2,1:T(8,128)} %get-tuple-element.356, f32[256,8]{0,1:T(8,128)S(1)} %get-tuple-element.339, pred[]{:T(512)S(6)} %compare.8, ...), kind=kOutput, calls=%fused_computation.12.clone.1 | convolution fusion | flops 273416192 | bytes 6569989 | tf_op jit(solution)/shard_map/while/body/eval_jaxpr/ihgk,khd->ihgd/dot_general | solution.py:22
  215.9 3.6 %fusion.142 = (f32[256,8]{0,1:T(8,128)S(1)}, f32[512,256,8]{1,0,2:T(8,128)}) fusion(pred[256,512]{0,1:T(8,128)(4,1)S(1)} %compare_select_fusion.2, bf16[256,1,8,128]{3,0,2,1:T(8,128)(2,1)S(1)} %get-tuple-element.373, bf16[6144,128]{1,0:T(8,128)(2,1)} %get-tuple-element.372, s32[]{:T(128)S(6)} %select_n.322), kind=kOutput, calls=%fused_computation.3.clone.1 | convolution fusion | flops 271579136 | bytes 4988932 | tf_op jit(solution)/shard_map/while/body/eval_jaxpr/ihgd,khd->ihgk/dot_general | solution.py:91
  219.6 4.8 %fusion.145 = f32[256,1,8,128]{0,3,2,1:T(8,128)} fusion(f32[512,256,8]{1,0,2:T(8,128)} %get-tuple-element.338, f32[256,8]{0,1:T(8,128)S(1)} %bitcast.375, pred[256,512]{0,1:T(8,128)(4,1)S(1)} %compare_select_fusion.2, f32[256,1,8,128]{0,3,2,1:T(8,128)} %get-tuple-element.356, f32[256,8]{0,1:T(8,128)S(1)} %get-tuple-element.339, pred[]{:T(512)S(6)} %compare.8, ...), kind=kOutput, calls=%fused_computation.12.clone.1 | convolution fusion | flops 273416192 | bytes 6569989 | tf_op jit(solution)/shard_map/while/body/eval_jaxpr/ihgk,khd->ihgd/dot_general | solution.py:22
  230.1 3.6 %fusion.142 = (f32[256,8]{0,1:T(8,128)S(1)}, f32[512,256,8]{1,0,2:T(8,128)}) fusion(pred[256,512]{0,1:T(8,128)(4,1)S(1)} %compare_select_fusion.2, bf16[256,1,8,128]{3,0,2,1:T(8,128)(2,1)S(1)} %get-tuple-element.373, bf16[6144,128]{1,0:T(8,128)(2,1)} %get-tuple-element.372, s32[]{:T(128)S(6)} %select_n.322), kind=kOutput, calls=%fused_computation.3.clone.1 | convolution fusion | flops 271579136 | bytes 4988932 | tf_op jit(solution)/shard_map/while/body/eval_jaxpr/ihgd,khd->ihgk/dot_general | solution.py:91
  233.8 4.8 %fusion.145 = f32[256,1,8,128]{0,3,2,1:T(8,128)} fusion(f32[512,256,8]{1,0,2:T(8,128)} %get-tuple-element.338, f32[256,8]{0,1:T(8,128)S(1)} %bitcast.375, pred[256,512]{0,1:T(8,128)(4,1)S(1)} %compare_select_fusion.2, f32[256,1,8,128]{0,3,2,1:T(8,128)} %get-tuple-element.356, f32[256,8]{0,1:T(8,128)S(1)} %get-tuple-element.339, pred[]{:T(512)S(6)} %compare.8, ...), kind=kOutput, calls=%fused_computation.12.clone.1 | convolution fusion | flops 273416192 | bytes 6569989 | tf_op jit(solution)/shard_map/while/body/eval_jaxpr/ihgk,khd->ihgd/dot_general | solution.py:22
  244.3 3.6 %fusion.142 = (f32[256,8]{0,1:T(8,128)S(1)}, f32[512,256,8]{1,0,2:T(8,128)}) fusion(pred[256,512]{0,1:T(8,128)(4,1)S(1)} %compare_select_fusion.2, bf16[256,1,8,128]{3,0,2,1:T(8,128)(2,1)S(1)} %get-tuple-element.373, bf16[6144,128]{1,0:T(8,128)(2,1)} %get-tuple-element.372, s32[]{:T(128)S(6)} %select_n.322), kind=kOutput, calls=%fused_computation.3.clone.1 | convolution fusion | flops 271579136 | bytes 4988932 | tf_op jit(solution)/shard_map/while/body/eval_jaxpr/ihgd,khd->ihgk/dot_general | solution.py:91
  248.0 4.8 %fusion.145 = f32[256,1,8,128]{0,3,2,1:T(8,128)} fusion(f32[512,256,8]{1,0,2:T(8,128)} %get-tuple-element.338, f32[256,8]{0,1:T(8,128)S(1)} %bitcast.375, pred[256,512]{0,1:T(8,128)(4,1)S(1)} %compare_select_fusion.2, f32[256,1,8,128]{0,3,2,1:T(8,128)} %get-tuple-element.356, f32[256,8]{0,1:T(8,128)S(1)} %get-tuple-element.339, pred[]{:T(512)S(6)} %compare.8, ...), kind=kOutput, calls=%fused_computation.12.clone.1 | convolution fusion | flops 273416192 | bytes 6569989 | tf_op jit(solution)/shard_map/while/body/eval_jaxpr/ihgk,khd->ihgd/dot_general | solution.py:22
  258.5 3.6 %fusion.142 = (f32[256,8]{0,1:T(8,128)S(1)}, f32[512,256,8]{1,0,2:T(8,128)}) fusion(pred[256,512]{0,1:T(8,128)(4,1)S(1)} %compare_select_fusion.2, bf16[256,1,8,128]{3,0,2,1:T(8,128)(2,1)S(1)} %get-tuple-element.373, bf16[6144,128]{1,0:T(8,128)(2,1)} %get-tuple-element.372, s32[]{:T(128)S(6)} %select_n.322), kind=kOutput, calls=%fused_computation.3.clone.1 | convolution fusion | flops 271579136 | bytes 4988932 | tf_op jit(solution)/shard_map/while/body/eval_jaxpr/ihgd,khd->ihgk/dot_general | solution.py:91
  262.2 4.8 %fusion.145 = f32[256,1,8,128]{0,3,2,1:T(8,128)} fusion(f32[512,256,8]{1,0,2:T(8,128)} %get-tuple-element.338, f32[256,8]{0,1:T(8,128)S(1)} %bitcast.375, pred[256,512]{0,1:T(8,128)(4,1)S(1)} %compare_select_fusion.2, f32[256,1,8,128]{0,3,2,1:T(8,128)} %get-tuple-element.356, f32[256,8]{0,1:T(8,128)S(1)} %get-tuple-element.339, pred[]{:T(512)S(6)} %compare.8, ...), kind=kOutput, calls=%fused_computation.12.clone.1 | convolution fusion | flops 273416192 | bytes 6569989 | tf_op jit(solution)/shard_map/while/body/eval_jaxpr/ihgk,khd->ihgd/dot_general | solution.py:22
  272.7 3.6 %fusion.142 = (f32[256,8]{0,1:T(8,128)S(1)}, f32[512,256,8]{1,0,2:T(8,128)}) fusion(pred[256,512]{0,1:T(8,128)(4,1)S(1)} %compare_select_fusion.2, bf16[256,1,8,128]{3,0,2,1:T(8,128)(2,1)S(1)} %get-tuple-element.373, bf16[6144,128]{1,0:T(8,128)(2,1)} %get-tuple-element.372, s32[]{:T(128)S(6)} %select_n.322), kind=kOutput, calls=%fused_computation.3.clone.1 | convolution fusion | flops 271579136 | bytes 4988932 | tf_op jit(solution)/shard_map/while/body/eval_jaxpr/ihgd,khd->ihgk/dot_general | solution.py:91
  276.4 4.8 %fusion.145 = f32[256,1,8,128]{0,3,2,1:T(8,128)} fusion(f32[512,256,8]{1,0,2:T(8,128)} %get-tuple-element.338, f32[256,8]{0,1:T(8,128)S(1)} %bitcast.375, pred[256,512]{0,1:T(8,128)(4,1)S(1)} %compare_select_fusion.2, f32[256,1,8,128]{0,3,2,1:T(8,128)} %get-tuple-element.356, f32[256,8]{0,1:T(8,128)S(1)} %get-tuple-element.339, pred[]{:T(512)S(6)} %compare.8, ...), kind=kOutput, calls=%fused_computation.12.clone.1 | convolution fusion | flops 273416192 | bytes 6569989 | tf_op jit(solution)/shard_map/while/body/eval_jaxpr/ihgk,khd->ihgd/dot_general | solution.py:22
  286.9 3.6 %fusion.142 = (f32[256,8]{0,1:T(8,128)S(1)}, f32[512,256,8]{1,0,2:T(8,128)}) fusion(pred[256,512]{0,1:T(8,128)(4,1)S(1)} %compare_select_fusion.2, bf16[256,1,8,128]{3,0,2,1:T(8,128)(2,1)S(1)} %get-tuple-element.373, bf16[6144,128]{1,0:T(8,128)(2,1)} %get-tuple-element.372, s32[]{:T(128)S(6)} %select_n.322), kind=kOutput, calls=%fused_computation.3.clone.1 | convolution fusion | flops 271579136 | bytes 4988932 | tf_op jit(solution)/shard_map/while/body/eval_jaxpr/ihgd,khd->ihgk/dot_general | solution.py:91
  290.6 4.8 %fusion.145 = f32[256,1,8,128]{0,3,2,1:T(8,128)} fusion(f32[512,256,8]{1,0,2:T(8,128)} %get-tuple-element.338, f32[256,8]{0,1:T(8,128)S(1)} %bitcast.375, pred[256,512]{0,1:T(8,128)(4,1)S(1)} %compare_select_fusion.2, f32[256,1,8,128]{0,3,2,1:T(8,128)} %get-tuple-element.356, f32[256,8]{0,1:T(8,128)S(1)} %get-tuple-element.339, pred[]{:T(512)S(6)} %compare.8, ...), kind=kOutput, calls=%fused_computation.12.clone.1 | convolution fusion | flops 273416192 | bytes 6569989 | tf_op jit(solution)/shard_map/while/body/eval_jaxpr/ihgk,khd->ihgd/dot_general | solution.py:22
  301.1 3.6 %fusion.142 = (f32[256,8]{0,1:T(8,128)S(1)}, f32[512,256,8]{1,0,2:T(8,128)}) fusion(pred[256,512]{0,1:T(8,128)(4,1)S(1)} %compare_select_fusion.2, bf16[256,1,8,128]{3,0,2,1:T(8,128)(2,1)S(1)} %get-tuple-element.373, bf16[6144,128]{1,0:T(8,128)(2,1)} %get-tuple-element.372, s32[]{:T(128)S(6)} %select_n.322), kind=kOutput, calls=%fused_computation.3.clone.1 | convolution fusion | flops 271579136 | bytes 4988932 | tf_op jit(solution)/shard_map/while/body/eval_jaxpr/ihgd,khd->ihgk/dot_general | solution.py:91
  304.8 4.8 %fusion.145 = f32[256,1,8,128]{0,3,2,1:T(8,128)} fusion(f32[512,256,8]{1,0,2:T(8,128)} %get-tuple-element.338, f32[256,8]{0,1:T(8,128)S(1)} %bitcast.375, pred[256,512]{0,1:T(8,128)(4,1)S(1)} %compare_select_fusion.2, f32[256,1,8,128]{0,3,2,1:T(8,128)} %get-tuple-element.356, f32[256,8]{0,1:T(8,128)S(1)} %get-tuple-element.339, pred[]{:T(512)S(6)} %compare.8, ...), kind=kOutput, calls=%fused_computation.12.clone.1 | convolution fusion | flops 273416192 | bytes 6569989 | tf_op jit(solution)/shard_map/while/body/eval_jaxpr/ihgk,khd->ihgd/dot_general | solution.py:22
  (234 shorter events, 58.8 us)
Async XLA Ops:
  7.2 74.8 %copy-start = (bf16[32,1,256,128]{3,2,1,0:T(8,128)(2,1)S(1)}, bf16[32,1,256,128]{3,2,1,0:T(8,128)(2,1)}, u32[]{:S(2)}) copy-start(bf16[32,1,256,128]{3,2,1,0:T(8,128)(2,1)} %param.22) | copy-start | bytes 6291460
  7.2 42.1 %copy-start.11 = (bf16[1,256,128]{2,1,0:T(8,128)(2,1)S(1)}, bf16[1,256,128]{2,1,0:T(8,128)(2,1)}, u32[]{:S(2)}) copy-start(bf16[1,256,128]{2,1,0:T(8,128)(2,1)} %param.19) | copy-start | bytes 196612
  7.2 41.3 %copy-start.10 = (bf16[1,256,128]{2,1,0:T(8,128)(2,1)S(1)}, bf16[1,256,128]{2,1,0:T(8,128)(2,1)}, u32[]{:S(2)}) copy-start(bf16[1,256,128]{2,1,0:T(8,128)(2,1)} %param.18) | copy-start | bytes 196612
  7.2 41.3 %copy-start.18 = (bf16[1,128,128]{2,1,0:T(8,128)(2,1)S(1)}, bf16[1,128,128]{2,1,0:T(8,128)(2,1)}, u32[]{:S(2)}) copy-start(bf16[1,128,128]{2,1,0:T(8,128)(2,1)} %param.16) | copy-start | bytes 98308
  7.2 61.9 %copy-start.25 = (s32[32]{0:T(128)S(1)}, s32[32]{0:T(128)}, u32[]{:S(2)}) copy-start(s32[32]{0:T(128)} %param.24) | copy-start | bytes 388
  7.2 133.2 %all-gather.7.cloned.1.call-start = ((), (), s32[]{:S(2)}) async-start(), calls=%async_computation.3 | async-start | bytes 1671168 | tf_op jit(solution)/shard_map/all_gather | solution.py:73
  9.2 60.1 %copy-start.26 = (s32[32]{0:T(128)S(1)}, s32[32]{0:T(128)}, u32[]{:S(2)}) copy-start(s32[32]{0:T(128)} %param.25) | copy-start | bytes 388
  10.9 70.8 %collective-permute-start.1 = (bf16[32,4,4,128]{3,2,1,0:T(4,128)(2,1)S(1)}, bf16[32,4,4,128]{3,2,1,0:T(4,128)(2,1)S(1)}, u32[]{:S(2)}, u32[]{:S(2)}) collective-permute-start(bf16[32,4,4,128]{3,2,1,0:T(4,128)(2,1)S(1)} %concatenate.58), channel_id=1, source_target_pairs={{0,8},{8,0},{16,24},{24,16},{32,40},{40,32},{48,56},{56,48},{64,72... | collective-permute-start | bytes 393224 | tf_op jit(solution)/shard_map/ppermute | solution.py:12
  36.9 33.4 %all-to-all-start = ((bf16[128,16,128]{2,0,1:T(8,128)(2,1)}), bf16[128,16,128]{2,0,1:T(8,128)(2,1)}, u32[]{:S(2)}, u32[]{:S(2)}) async-start(bf16[128,16,128]{2,0,1:T(8,128)(2,1)} %bitcast.9), calls=%async_computation | async-start | bytes 1048576 | tf_op jit(solution)/shard_map/all_to_all | solution.py:147
  48.5 92.0 %all-gather.5.cloned.1.call-start = ((), (), s32[]{:S(2)}) async-start(), calls=%async_computation.2 | async-start | bytes 1671168 | tf_op jit(solution)/shard_map/all_gather | solution.py:72
  69.2 17.1 %copy-start.16 = (pred[32,256]{1,0:T(8,128)(4,1)}, pred[32,256]{1,0:T(8,128)(4,1)S(1)}, u32[]{:S(2)}) copy-start(pred[32,256]{1,0:T(8,128)(4,1)S(1)} %broadcast_compare_fusion.1) | copy-start | bytes 24580
  69.4 33.4 %copy-start.19 = (pred[32]{0:T(512)(128)(4,1)}, pred[32]{0:T(512)(128)(4,1)S(1)}, u32[]{:S(2)}) copy-start(pred[32]{0:T(512)(128)(4,1)S(1)} %get-tuple-element.253) | copy-start | bytes 100
  69.4 35.0 %copy-start.22 = (pred[32]{0:T(512)(128)(4,1)}, pred[32]{0:T(512)(128)(4,1)S(1)}, u32[]{:S(2)}) copy-start(pred[32]{0:T(512)(128)(4,1)S(1)} %get-tuple-element.254) | copy-start | bytes 100
  70.3 22.9 %all-to-all-start.1 = ((bf16[128,16,128]{2,0,1:T(8,128)(2,1)}), bf16[128,16,128]{2,0,1:T(8,128)(2,1)}, u32[]{:S(2)}, u32[]{:S(2)}) async-start(bf16[128,16,128]{2,0,1:T(8,128)(2,1)} %bitcast.22), calls=%async_computation.1 | async-start | bytes 1048576 | tf_op jit(solution)/shard_map/all_to_all | solution.py:148
  81.2 19.9 %collective-permute-start = (bf16[2048,1,128]{2,0,1:T(8,128)(2,1)}, bf16[2048,1,128]{2,0,1:T(8,128)(2,1)}, u32[]{:S(2)}, u32[]{:S(2)}) collective-permute-start(bf16[2048,1,128]{2,0,1:T(8,128)(2,1)} %bitcast.14), channel_id=1, source_target_pairs={{0,128},{128,0},{1,129},{129,1},{2,130},{130,2},{3,131},{131,3},{4... | collective-permute-start | bytes 1572872 | tf_op jit(solution)/shard_map/ppermute | solution.py:12
  81.7 22.7 %copy-start.23 = (pred[4,4]{1,0:T(4,128)(4,1)}, pred[4,4]{1,0:T(4,128)(4,1)S(1)}, u32[]{:S(2)}) copy-start(pred[4,4]{1,0:T(4,128)(4,1)S(1)} %fusion.120) | copy-start | bytes 52
  93.3 23.9 %collective-permute-start.2 = (bf16[2048,1,128]{2,0,1:T(8,128)(2,1)}, bf16[2048,1,128]{2,0,1:T(8,128)(2,1)}, u32[]{:S(2)}, u32[]{:S(2)}) collective-permute-start(bf16[2048,1,128]{2,0,1:T(8,128)(2,1)} %bitcast.27), channel_id=1, source_target_pairs={{0,128},{128,0},{1,129},{129,1},{2,130},{130,2},{3,131},{131,3},{4... | collective-permute-start | bytes 1572872 | tf_op jit(solution)/shard_map/ppermute | solution.py:12
  104.3 3.3 %copy-start.2 = (f32[2048,32,4,8]{0,1,3,2:T(8,128)}, f32[2048,32,4,8]{0,1,3,2:T(8,128)S(1)}, u32[]{:S(2)}) copy-start(f32[2048,32,4,8]{0,1,3,2:T(8,128)S(1)} %get-tuple-element.260) | copy-start | bytes 25165828
  104.4 3.3 %copy-start.20 = (pred[32]{0:T(512)(128)(4,1)S(1)}, pred[32]{0:T(512)(128)(4,1)}, u32[]{:S(2)}) copy-start(pred[32]{0:T(512)(128)(4,1)} %copy-done.19) | copy-start | bytes 100
  105.9 6.7 %copy-start.3 = (f32[2048,32,4,8]{0,1,3,2:T(8,128)}, f32[2048,32,4,8]{0,1,3,2:T(8,128)S(1)}, u32[]{:S(2)}) copy-start(f32[2048,32,4,8]{0,1,3,2:T(8,128)S(1)} %get-tuple-element.262) | copy-start | bytes 25165828
  105.9 6.7 %copy-start.15 = (f32[32,4,8]{0,2,1:T(8,128)}, f32[32,4,8]{0,2,1:T(8,128)S(1)}, u32[]{:S(2)}) copy-start(f32[32,4,8]{0,2,1:T(8,128)S(1)} %get-tuple-element.261) | copy-start | bytes 12292
  107.1 5.5 %copy-start.13 = (f32[32,4,8]{0,2,1:T(8,128)}, f32[32,4,8]{0,2,1:T(8,128)S(1)}, u32[]{:S(2)}) copy-start(f32[32,4,8]{0,2,1:T(8,128)S(1)} %get-tuple-element.236) | copy-start | bytes 12292
  107.1 5.5 %copy-start.17 = (f32[32,4,8]{0,2,1:T(8,128)}, f32[32,4,8]{0,2,1:T(8,128)S(1)}, u32[]{:S(2)}) copy-start(f32[32,4,8]{0,2,1:T(8,128)S(1)} %get-tuple-element.252) | copy-start | bytes 12292
  107.1 5.5 %copy-start.12 = (f32[32,4,8]{0,2,1:T(8,128)}, f32[32,4,8]{0,2,1:T(8,128)S(1)}, u32[]{:S(2)}) copy-start(f32[32,4,8]{0,2,1:T(8,128)S(1)} %get-tuple-element.235) | copy-start | bytes 12292
  107.6 5.9 %copy-start.6 = (f32[32,4,1,8,4]{3,4,1,0,2:T(4,128)S(1)}, f32[32,4,1,8,4]{3,4,1,0,2:T(4,128)}, u32[]{:S(2)}) copy-start(f32[32,4,1,8,4]{3,4,1,0,2:T(4,128)} %get-tuple-element.256) | copy-start | bytes 49156
  112.8 7.1 %copy-start.4 = (bf16[32,1,256,128]{3,2,1,0:T(8,128)(2,1)S(1)}, bf16[32,1,256,128]{3,2,1,0:T(8,128)(2,1)}, u32[]{:S(2)}) copy-start(bf16[32,1,256,128]{3,2,1,0:T(8,128)(2,1)} %param.23) | copy-start | bytes 6291460
  112.8 9.1 %copy-start.24 = (pred[4,4]{1,0:T(4,128)(4,1)S(1)}, pred[4,4]{1,0:T(4,128)(4,1)}, u32[]{:S(2)}) copy-start(pred[4,4]{1,0:T(4,128)(4,1)} %copy-done.23) | copy-start | bytes 52
  112.8 10.4 %collective-permute-start.3 = (bf16[32,4,8]{0,2,1:T(8,128)(2,1)}, bf16[32,4,8]{0,2,1:T(8,128)(2,1)}, u32[]{:S(2)}, u32[]{:S(2)}) collective-permute-start(bf16[32,4,8]{0,2,1:T(8,128)(2,1)} %get-tuple-element.233), channel_id=1, source_target_pairs={{0,8},{8,0},{16,24},{24,16},{32,40},{40,32},{48,56},{56,48},{64,72... | collective-permute-start | bytes 6152 | tf_op jit(solution)/shard_map/ppermute | solution.py:12
  124.7 5.1 %copy-start.5 = (bf16[2,2048,1,128]{3,1,2,0:T(8,128)(2,1)S(1)}, bf16[2,2048,1,128]{3,1,2,0:T(8,128)(2,1)}, u32[]{:S(2)}) copy-start(bf16[2,2048,1,128]{3,1,2,0:T(8,128)(2,1)} %maximum_select_fusion.1) | copy-start | bytes 3145732
  124.7 5.1 %copy-start.7 = (f32[32,4,8,128]{3,2,1,0:T(8,128)S(1)}, f32[32,4,8,128]{3,2,1,0:T(8,128)}, u32[]{:S(2)}) copy-start(f32[32,4,8,128]{3,2,1,0:T(8,128)} %fusion.47) | copy-start | bytes 1572868
  124.7 5.1 %copy-start.9 = (f32[32,128,4,8]{1,3,2,0:T(8,128)S(1)}, f32[32,128,4,8]{1,3,2,0:T(8,128)}, u32[]{:S(2)}) copy-start(f32[32,128,4,8]{1,3,2,0:T(8,128)} %fusion.106) | copy-start | bytes 1572868
  124.7 5.2 %copy-start.14 = (f32[32,4,8]{0,2,1:T(8,128)S(1)}, f32[32,4,8]{0,2,1:T(8,128)}, u32[]{:S(2)}) copy-start(f32[32,4,8]{0,2,1:T(8,128)} %copy-done.13) | copy-start | bytes 12292
  124.7 5.2 %copy-start.21 = (pred[32]{0:T(512)(128)(4,1)S(1)}, pred[32]{0:T(512)(128)(4,1)}, u32[]{:S(2)}) copy-start(pred[32]{0:T(512)(128)(4,1)} %copy-done.19) | copy-start | bytes 100
  129.8 7.3 %copy-start.8 = (bf16[1,256,1024]{2,1,0:T(8,128)(2,1)S(1)}, bf16[1,256,1024]{2,1,0:T(8,128)(2,1)}, u32[]{:S(2)}) copy-start(bf16[1,256,1024]{2,1,0:T(8,128)(2,1)} %param.15) | copy-start | bytes 1572868
  136.6 1.8 collective-permute-start.4
  136.9 1.5 collective-permute-start.5
  148.9 4.5 %copy-start.1 = (f32[512,256,8]{1,0,2:T(8,128)S(1)}, f32[512,256,8]{1,0,2:T(8,128)}, u32[]{:S(2)}) copy-start(f32[512,256,8]{1,0,2:T(8,128)} %get-tuple-element.338) | copy-start | bytes 12582916 | tf_op jit(solution)/shard_map/while
  162.8 4.8 %copy-start.1 = (f32[512,256,8]{1,0,2:T(8,128)S(1)}, f32[512,256,8]{1,0,2:T(8,128)}, u32[]{:S(2)}) copy-start(f32[512,256,8]{1,0,2:T(8,128)} %get-tuple-element.338) | copy-start | bytes 12582916 | tf_op jit(solution)/shard_map/while
  177.0 4.8 %copy-start.1 = (f32[512,256,8]{1,0,2:T(8,128)S(1)}, f32[512,256,8]{1,0,2:T(8,128)}, u32[]{:S(2)}) copy-start(f32[512,256,8]{1,0,2:T(8,128)} %get-tuple-element.338) | copy-start | bytes 12582916 | tf_op jit(solution)/shard_map/while
  191.2 4.8 %copy-start.1 = (f32[512,256,8]{1,0,2:T(8,128)S(1)}, f32[512,256,8]{1,0,2:T(8,128)}, u32[]{:S(2)}) copy-start(f32[512,256,8]{1,0,2:T(8,128)} %get-tuple-element.338) | copy-start | bytes 12582916 | tf_op jit(solution)/shard_map/while
  205.4 4.8 %copy-start.1 = (f32[512,256,8]{1,0,2:T(8,128)S(1)}, f32[512,256,8]{1,0,2:T(8,128)}, u32[]{:S(2)}) copy-start(f32[512,256,8]{1,0,2:T(8,128)} %get-tuple-element.338) | copy-start | bytes 12582916 | tf_op jit(solution)/shard_map/while
  219.6 4.8 %copy-start.1 = (f32[512,256,8]{1,0,2:T(8,128)S(1)}, f32[512,256,8]{1,0,2:T(8,128)}, u32[]{:S(2)}) copy-start(f32[512,256,8]{1,0,2:T(8,128)} %get-tuple-element.338) | copy-start | bytes 12582916 | tf_op jit(solution)/shard_map/while
  233.8 4.8 %copy-start.1 = (f32[512,256,8]{1,0,2:T(8,128)S(1)}, f32[512,256,8]{1,0,2:T(8,128)}, u32[]{:S(2)}) copy-start(f32[512,256,8]{1,0,2:T(8,128)} %get-tuple-element.338) | copy-start | bytes 12582916 | tf_op jit(solution)/shard_map/while
  248.0 4.8 %copy-start.1 = (f32[512,256,8]{1,0,2:T(8,128)S(1)}, f32[512,256,8]{1,0,2:T(8,128)}, u32[]{:S(2)}) copy-start(f32[512,256,8]{1,0,2:T(8,128)} %get-tuple-element.338) | copy-start | bytes 12582916 | tf_op jit(solution)/shard_map/while
  262.2 4.8 %copy-start.1 = (f32[512,256,8]{1,0,2:T(8,128)S(1)}, f32[512,256,8]{1,0,2:T(8,128)}, u32[]{:S(2)}) copy-start(f32[512,256,8]{1,0,2:T(8,128)} %get-tuple-element.338) | copy-start | bytes 12582916 | tf_op jit(solution)/shard_map/while
  276.4 4.8 %copy-start.1 = (f32[512,256,8]{1,0,2:T(8,128)S(1)}, f32[512,256,8]{1,0,2:T(8,128)}, u32[]{:S(2)}) copy-start(f32[512,256,8]{1,0,2:T(8,128)} %get-tuple-element.338) | copy-start | bytes 12582916 | tf_op jit(solution)/shard_map/while
  290.6 4.8 %copy-start.1 = (f32[512,256,8]{1,0,2:T(8,128)S(1)}, f32[512,256,8]{1,0,2:T(8,128)}, u32[]{:S(2)}) copy-start(f32[512,256,8]{1,0,2:T(8,128)} %get-tuple-element.338) | copy-start | bytes 12582916 | tf_op jit(solution)/shard_map/while
  304.8 4.8 %copy-start.1 = (f32[512,256,8]{1,0,2:T(8,128)S(1)}, f32[512,256,8]{1,0,2:T(8,128)}, u32[]{:S(2)}) copy-start(f32[512,256,8]{1,0,2:T(8,128)} %get-tuple-element.338) | copy-start | bytes 12582916 | tf_op jit(solution)/shard_map/while
Sparse Core Ops, SparseCore 0:
  10.7 58.1 all-gather.6
  71.6 52.3 all-gather.4
where the time goes:
time: 321 us; the launch traced here: 320 us
  matrix products  124 us (39%)
  other arithmetic  56.1 us (17%)
  blocking collectives  41.5 us (13%)
  starting transfers between devices  27.5 us (9%)
  loops' own time  24 us (7%)
  local copies, waits for them, and re-layouts  17.1 us (5%)
  waiting for transfers between devices  14.7 us (5%)
  between operations  14.5 us (5%)
    dot_general x16, matrix products, online_update(): jnp.einsum(form, weights.astype(jnp.bfloat16), value_rows, preferred_elem...  73.1 us
    dot_general x12, matrix products, one_block(): jnp.einsum('ihgd,khd->ihgk', query_four, key_rows, preferred_element_type...  43.8 us
    another operation x1, loops' own time, local(): top, total, summed = lax.scan(one_block, start_state, offsets)[0]  24 us
    all_gather x1, blocking collectives, local(): lax.all_gather(document_key[0], 'rep', axis=1, tiled=True)  21.7 us
    all_gather x1, blocking collectives, local(): lax.all_gather(document_value[0], 'rep', axis=1, tiled=True)  19.9 us
    reduce_sum x15, other arithmetic, online_update(): total = total * factor + jnp.sum(weights, axis=-1)  17.6 us
    lt x12, other arithmetic, one_block(): hist_ok = shard * hist_rows + within < start_slot  15.7 us
    all_to_all x1, starting transfers between devices, local(): lax.all_to_all(run_key, 'seq', split_axis=1, concat_axis=0, tiled=True)  11.6 us
  transfers between devices with their start and end apart: 10, of which 3 were waited for; matrix products, arithmetic and copies ran while one was open for 14% of the time, Pallas kernels for 0%

commit v1 on v0

v1 whole, which is shorter than its diff:
```python
import functools

import jax
import jax.numpy as jnp
from jax import lax
from jax.experimental import pallas as pl
from jax.experimental.pallas import tpu as pltpu
from jax.sharding import PartitionSpec as P

HEAD = 128
LOG2E = 1.4426950408889634
SCALE = HEAD ** (-0.5) * LOG2E
LOW = -1e30
F32 = jnp.float32
BF16 = jnp.bfloat16
MESH = pl.DeviceIdType.MESH
NT = (((1,), (1,)), ((), ()))
NN = (((1,), (0,)), ((), ()))


def kernel(
    pre_query,
    hist_key,
    hist_value,
    doc_key,
    doc_value,
    start_ref,
    dec_query,
    cache_key,
    cache_value,
    length_ref,
    owner_ref,
    new_key,
    new_value,
    pre_out,
    dec_out,
    buf,
    vals,
    pre_q,
    pre_raw,
    pre_o,
    q_own,
    q_sib,
    ck,
    cv,
    kn,
    vn,
    o_own,
    l_own,
    o_snd,
    l_snd,
    o_sib,
    l_sib,
    dq,
    od_snd,
    ld_snd,
    od,
    ld,
    dec_o,
    s0,
    s1,
    s2,
    acc,
    tot,
    mrun,
    macc,
    dacc,
    dtot,
    dmrun,
    dmacc,
    in_sem,
    out_sem,
    send_sem,
    r0,
    r1,
    rx,
):
    grp = lax.axis_index("grp")
    seq = lax.axis_index("seq")
    rep = lax.axis_index("rep")
    y, xh, core = seq // 4, (seq // 2) % 2, seq % 2
    run = core
    chip = seq // 2

    def seq_at(dy, other):
        return ((y + dy) % 4) * 4 + (xh + other) % 2 * 2 + core

    up = {"seq": seq_at(1, 0)}
    down = {"seq": seq_at(3, 0)}
    across = {"seq": seq_at(0, 1)}
    sib = {"seq": seq + 1 - 2 * core}
    doc_seq = ((rep + 1) % 8) * 2 + grp
    doc_dev = [{"grp": g, "seq": doc_seq, "rep": chip} for g in range(2)]
    src_rep = (chip + 7) % 8
    src_dev = [{"grp": core, "seq": 2 * rep + i, "rep": src_rep} for i in range(2)]

    loads = [
        pltpu.make_async_copy(hist_key, buf.at[seq, pl.ds(0, 128)], in_sem.at[0]),
        pltpu.make_async_copy(doc_key, buf.at[seq, pl.ds(128, 256)], in_sem.at[1]),
        pltpu.make_async_copy(hist_value, vals.at[pl.ds(0, 128)], in_sem.at[2]),
        pltpu.make_async_copy(doc_value, vals.at[pl.ds(128, 256)], in_sem.at[3]),
        pltpu.make_async_copy(dec_query, q_own, in_sem.at[4]),
        pltpu.make_async_copy(cache_key, ck, in_sem.at[5]),
        pltpu.make_async_copy(cache_value, cv, in_sem.at[6]),
        pltpu.make_async_copy(pre_query, pre_raw, in_sem.at[7]),
        pltpu.make_async_copy(new_key, kn, in_sem.at[8]),
        pltpu.make_async_copy(new_value, vn, in_sem.at[9]),
    ]
    for c in loads:
        c.start()

    barrier = pltpu.get_barrier_semaphore()
    partners = [up, down, across, sib] + doc_dev + src_dev
    for d in partners:
        pl.semaphore_signal(barrier, inc=1, device_id=d, device_id_type=MESH)

    for c in loads[:4]:
        c.wait()
    for i in range(3):
        v = vals[i * 128 : (i + 1) * 128, :]
        buf[seq, 384 + i * 128 : 512 + i * 128, :] = v.astype(F32).T.astype(BF16)
    loads[4].wait()
    pl.semaphore_wait(barrier, len(partners))

    sends = []

    def send(src, dst, recv, dev):
        c = pltpu.make_async_remote_copy(
            src_ref=src,
            dst_ref=dst,
            send_sem=send_sem.at[len(sends)],
            recv_sem=recv,
            device_id=dev,
            device_id_type=MESH,
        )
        c.start()
        sends.append(c)

    def arrived(dst, recv):
        pltpu.make_async_remote_copy(
            src_ref=dst,
            dst_ref=dst,
            send_sem=send_sem.at[0],
            recv_sem=recv,
            device_id=sib,
            device_id_type=MESH,
        ).wait_recv()

    first, second = pl.ds(0, 384), pl.ds(384, 384)

    def send_block(b, dev):
        send(buf.at[b], buf.at[b], r0.at[b], dev)

    def send_first(b, dev):
        send(buf.at[b, first], buf.at[b, first], r0.at[b], dev)

    def send_second(b, dev):
        send(buf.at[b, second], buf.at[b, second], r1.at[b], dev)

    def block_in(b):
        arrived(buf.at[b], r0.at[b])

    def halves_in(b):
        arrived(buf.at[b, first], r0.at[b])
        arrived(buf.at[b, second], r1.at[b])

    send(q_own, q_sib, rx.at[0], sib)
    send_block(seq, across)
    send_block(seq, up)
    send_block(seq, down)
    send_block(seq, sib)
    for g in range(2):
        send(q_own, dq.at[pl.ds(run * 512, 512)], rx.at[1 + run], doc_dev[g])

    def cache_rows(group, _):
        for i in range(4):
            r = group * 4 + i
            rows = pl.ds(pl.multiple_of(r * 16, 16), 16)
            q = jnp.concatenate([q_own[rows, :], q_sib[rows, :]], axis=0)
            s = lax.dot_general(q, ck[r], NT, preferred_element_type=F32)
            at = run * 256 + lax.broadcasted_iota(jnp.int32, (32, 256), 1)
            seen = at < length_ref[r]
            s = jnp.where(seen, s, LOW)
            m = jnp.max(s, axis=1, keepdims=True)
            p = jnp.where(seen, jnp.exp2(s - m), 0.0)
            l = jnp.sum(p, axis=1, keepdims=True)
            o = lax.dot_general(p.astype(BF16), cv[r], NN, preferred_element_type=F32)
            safe = jnp.maximum(l, 1e-30)
            o = o / safe
            top = jnp.where(l > 0.0, m + jnp.log(safe) * LOG2E, LOW)
            top = jnp.broadcast_to(top, (32, 128))
            o_own[rows, :] = o[:16]
            l_own[rows, :] = top[:16]
            o_snd[rows, :] = o[16:].astype(BF16)
            l_snd[rows, :] = top[16:]
        return 0

    arrived(q_sib, rx.at[0])
    loads[5].wait()
    loads[6].wait()
    lax.fori_loop(0, 4, cache_rows, 0)

    block_in(seq_at(0, 1))
    send_block(seq_at(0, 1), up)
    send_block(seq_at(0, 1), down)
    send_block(seq_at(0, 1), sib)
    block_in(seq_at(3, 0))
    send_first(seq_at(3, 0), up)
    send_block(seq_at(3, 0), sib)
    block_in(seq_at(1, 0))
    send_second(seq_at(1, 0), down)
    send_block(seq_at(1, 0), sib)

    lax.fori_loop(4, 8, cache_rows, 0)
    send(o_snd, o_sib, rx.at[3], sib)
    send(l_snd, l_sib, rx.at[4], sib)

    loads[7].wait()
    for h in range(8):
        x = pre_raw[:, h * 128 : (h + 1) * 128].astype(F32) * SCALE
        pre_q[h * 256 : (h + 1) * 256, :] = x.astype(BF16)

    acc[...] = jnp.zeros_like(acc)
    tot[...] = jnp.zeros_like(tot)
    mrun[...] = jnp.full_like(mrun, LOW)
    macc[...] = jnp.full_like(macc, LOW)

    def hist_keys(row):
        return jnp.concatenate([buf[row * 4 + c, 0:128, :] for c in range(4)], axis=0)

    def hist_vals(row):
        return jnp.concatenate([buf[row * 4 + c, 384:512, :] for c in range(4)], axis=1)

    def doc_keys(c):
        return jnp.concatenate([buf[c * 2 + i, 128:384, :] for i in range(2)], axis=0)

    def doc_vals(c):
        parts = [buf[c * 2 + i, 512 + 128 * j : 640 + 128 * j, :] for i in range(2) for j in range(2)]
        return jnp.concatenate(parts, axis=1)

    def score(q, keys, out, top, mask=None):
        lanes = q.shape[0]
        s = lax.dot_general(keys, q[...], NT, preferred_element_type=F32)
        if mask is not None:
            s = mask(s)
        out[:, :lanes] = s
        return jnp.maximum(top, jnp.max(s.reshape(64, 8, lanes), axis=0))

    def weigh(s, vals_t, m, state):
        a, t, ma = state
        lanes = a.shape[1]
        now = jnp.max(m, axis=0, keepdims=True)
        before = jnp.max(ma[...], axis=0, keepdims=True)
        f = jnp.exp2(before - now)
        p = jnp.exp2(s[:, :lanes] - now)
        t[...] = t[...] * f + jnp.sum(p.reshape(64, 8, lanes), axis=0)
        a[...] = a[...] * f + lax.dot_general(
            vals_t, p.astype(BF16), NN, preferred_element_type=F32
        )
        ma[...] = m

    pre_state = (acc, tot, macc)

    def hist_mask(row):
        def mask(s):
            slot = row * 512 + lax.broadcasted_iota(jnp.int32, (512, 128), 0)
            bias = jnp.where(slot < start_ref[0], 0.0, LOW)
            return s + jnp.concatenate([bias] * 16, axis=1)

        return mask

    def causal_mask(s):
        key_at = lax.broadcasted_iota(jnp.int32, s.shape, 0)
        query_at = core * 256 + (lax.broadcasted_iota(jnp.int32, s.shape, 1) & 255)
        return jnp.where(key_at <= query_at, s, LOW)

    def step(keys, out, mask, s, vals_t):
        m = mrun[...]
        new = score(pre_q, keys, out, m, mask)
        weigh(s, vals_t, m, pre_state)
        mrun[...] = new

    block_in(seq + 1 - 2 * core)
    mrun[...] = score(pre_q, doc_keys(chip), s1, mrun[...], causal_mask)
    block_in(((y * 4) + (1 - xh) * 2) + 1 - core)

    @pl.when(xh == 1)
    def _():
        step(doc_keys(y * 2), s2, None, s1, doc_vals(chip))
        step(hist_keys(y), s0, hist_mask(y), s2, doc_vals(y * 2))

    @pl.when(xh == 0)
    def _():
        step(hist_keys(y), s0, hist_mask(y), s1, doc_vals(chip))

    block_in(seq_at(3, 1))
    send_first(seq_at(3, 1), up)
    send_block(seq_at(3, 1), sib)
    block_in(seq_at(1, 1))
    send_second(seq_at(1, 1), down)
    send_block(seq_at(1, 1), sib)

    def other_in(row):
        for x in range(2):
            block_in(row * 4 + x * 2 + 1 - core)

    def row_step(row, last):
        @pl.when(row < y)
        def _():
            step(doc_keys(row * 2), s1, None, s0, hist_vals(last))
            step(doc_keys(row * 2 + 1), s2, None, s1, doc_vals(row * 2))
            step(hist_keys(row), s0, hist_mask(row), s2, doc_vals(row * 2 + 1))

        @pl.when(row > y)
        def _():
            weigh(s0, hist_vals(last), mrun[...], pre_state)
            mrun[...] = score(pre_q, hist_keys(row), s0, mrun[...], hist_mask(row))

    def row_of(k):
        return (y + jnp.where(k == 0, 0, jnp.where(k == 1, 3, k - 1))) % 4

    def near_row(k, _):
        row = row_of(k)
        other_in(row)
        row_step(row, row_of(k - 1))
        return 0

    lax.fori_loop(1, 3, near_row, 0)

    for x in range(2):
        halves_in(seq_at(2, x))
        send_block(seq_at(2, x), sib)
    other_in((y + 2) % 4)

    for i in range(2):
        arrived(dq.at[pl.ds(i * 512, 512)], rx.at[1 + i])
    dec_state = (dacc, dtot, dmacc)
    dacc[...] = jnp.zeros_like(dacc)
    dtot[...] = jnp.zeros_like(dtot)
    dmacc[...] = jnp.full_like(dmacc, LOW)
    dmrun[...] = score(dq, doc_keys(0), s1, jnp.full(dmrun.shape, LOW, F32))

    def doc_pair(j, _):
        m = dmrun[...]
        new = score(dq, doc_keys(2 * j + 1), s2, m)
        weigh(s1, doc_vals(2 * j), m, dec_state)
        last = score(dq, doc_keys((2 * j + 2) % 8), s1, new)
        weigh(s2, doc_vals(2 * j + 1), new, dec_state)
        dmrun[...] = last
        return 0

    lax.fori_loop(0, 4, doc_pair, 0)
    total = jnp.sum(dtot[...], axis=0, keepdims=True)
    level = jnp.max(dmacc[...], axis=0, keepdims=True) + jnp.log(total) * LOG2E
    level = jnp.broadcast_to(level, (8, 1024))
    for i in range(2):
        ld_snd[i] = level[:, i * 512 : (i + 1) * 512]
    od_snd[...] = (dacc[...] / total).T.astype(BF16)
    for i in range(2):
        send(od_snd.at[pl.ds(i * 512, 512)], od.at[grp], rx.at[5 + grp], src_dev[i])
        send(ld_snd.at[i], ld.at[grp], rx.at[7 + grp], src_dev[i])

    row_step((y + 2) % 4, (y + 1) % 4)
    weigh(s0, hist_vals((y + 2) % 4), mrun[...], pre_state)
    total = jnp.sum(tot[...], axis=0, keepdims=True)
    for h in range(8):
        cols = slice(h * 256, (h + 1) * 256)
        o = acc[:, cols] / total[:, cols]
        pre_o[:, h * 128 : (h + 1) * 128] = o.T.astype(BF16)
    pre_copy = pltpu.make_async_copy(pre_o, pre_out, out_sem.at[0])
    pre_copy.start()

    loads[8].wait()
    loads[9].wait()
    arrived(o_sib, rx.at[3])
    arrived(l_sib, rx.at[4])
    for g in range(2):
        arrived(od.at[g], rx.at[5 + g])
        arrived(ld.at[g], rx.at[7 + g])
    for c in range(4):
        rows = slice(c * 128, (c + 1) * 128)
        own_doc = jnp.concatenate(
            [jnp.full((16, 128), owner_ref[c * 8 + i], jnp.int32) for i in range(8)], axis=0
        )
        is_first = own_doc == 0
        levels = [jnp.broadcast_to(ld[g, 0:1, rows], (128, 128)).T for g in range(2)]
        l_doc = jnp.where(is_first, levels[0], levels[1])
        o_doc = jnp.where(is_first, od[0, rows, :].astype(F32), od[1, rows, :].astype(F32))
        s = lax.dot_general(q_own[rows, :], kn[...], NT, preferred_element_type=F32)
        line = c * 128 + lax.broadcasted_iota(jnp.int32, (128, 128), 0)
        col = lax.broadcasted_iota(jnp.int32, (128, 128), 1)
        seen = ((line >> 4) == (col >> 2)) & ((col & 3) <= ((line >> 2) & 3))
        s = jnp.where(seen, s, LOW)
        m = jnp.max(s, axis=1, keepdims=True)
        top = jnp.maximum(jnp.maximum(l_doc, l_own[rows, :]), jnp.maximum(l_sib[rows, :], m))
        p = jnp.where(seen, jnp.exp2(s - top), 0.0)
        w_doc = jnp.exp2(l_doc - top)
        w_own = jnp.exp2(l_own[rows, :] - top)
        w_sib = jnp.exp2(l_sib[rows, :] - top)
        o = lax.dot_general(p.astype(BF16), vn[...], NN, preferred_element_type=F32)
        o = o + w_doc * o_doc + w_own * o_own[rows, :] + w_sib * o_sib[rows, :].astype(F32)
        weight = jnp.sum(p, axis=1, keepdims=True) + w_doc + w_own + w_sib
        dec_o[rows, :] = (o / weight).astype(BF16)
    dec_copy = pltpu.make_async_copy(dec_o, dec_out, out_sem.at[1])
    dec_copy.start()
    for c in sends:
        c.wait_send()
    pre_copy.wait()
    dec_copy.wait()


def local(
    pre_query,
    history_key,
    history_value,
    document_key,
    document_value,
    stretch_start,
    decode_query,
    cached_row_keys,
    cached_row_values,
    cache_lengths,
    doc_owner,
    decode_key,
    decode_value,
):
    seq = lax.axis_index("seq")
    scaled = (decode_query.reshape(32, 4, 4, HEAD).astype(F32) * SCALE).astype(BF16)
    dec_q = scaled.reshape(512, HEAD)
    at = seq // 2 * HEAD
    new_key = lax.dynamic_slice_in_dim(decode_key, at, HEAD, 2).reshape(128, HEAD)
    new_value = lax.dynamic_slice_in_dim(decode_value, at, HEAD, 2).reshape(128, HEAD)
    smem = pl.BlockSpec(memory_space=pltpu.SMEM)
    hbm = pl.BlockSpec(memory_space=pl.ANY)

    def vm(shape, dtype):
        return pltpu.VMEM(shape, dtype)

    pre, dec = pl.pallas_call(
        kernel,
        out_shape=(
            jax.ShapeDtypeStruct((256, 1024), BF16),
            jax.ShapeDtypeStruct((512, 128), BF16),
        ),
        in_specs=[hbm, hbm, hbm, hbm, hbm, smem, hbm, hbm, hbm, smem, smem, hbm, hbm],
        out_specs=(hbm, hbm),
        scratch_shapes=[
            vm((16, 768, 128), BF16),
            vm((384, 128), BF16),
            vm((2048, 128), BF16),
            vm((256, 1024), BF16),
            vm((256, 1024), BF16),
            vm((512, 128), BF16),
            vm((512, 128), BF16),
            vm((32, 256, 128), BF16),
            vm((32, 256, 128), BF16),
            vm((128, 128), BF16),
            vm((128, 128), BF16),
            vm((512, 128), F32),
            vm((512, 128), F32),
            vm((512, 128), BF16),
            vm((512, 128), F32),
            vm((512, 128), BF16),
            vm((512, 128), F32),
            vm((1024, 128), BF16),
            vm((1024, 128), BF16),
            vm((2, 8, 512), F32),
            vm((2, 512, 128), BF16),
            vm((2, 8, 512), F32),
            vm((512, 128), BF16),
            vm((512, 2048), F32),
            vm((512, 2048), F32),
            vm((512, 2048), F32),
            vm((128, 2048), F32),
            vm((8, 2048), F32),
            vm((8, 2048), F32),
            vm((8, 2048), F32),
            vm((128, 1024), F32),
            vm((8, 1024), F32),
            vm((8, 1024), F32),
            vm((8, 1024), F32),
            pltpu.SemaphoreType.DMA((10,)),
            pltpu.SemaphoreType.DMA((2,)),
            pltpu.SemaphoreType.DMA((32,)),
            pltpu.SemaphoreType.DMA((16,)),
            pltpu.SemaphoreType.DMA((16,)),
            pltpu.SemaphoreType.DMA((9,)),
        ],
        compiler_params=pltpu.CompilerParams(
            collective_id=0, has_side_effects=True, vmem_limit_bytes=56 * 1024 * 1024
        ),
        name="attention",
    )(
        pre_query[0],
        history_key[0],
        history_value[0],
        document_key[0],
        document_value[0],
        stretch_start,
        dec_q,
        cached_row_keys.reshape(32, 256, HEAD),
        cached_row_values.reshape(32, 256, HEAD),
        cache_lengths,
        doc_owner,
        new_key,
        new_value,
    )
    return pre[None], dec.reshape(32, 4, 512)


def solution(mesh):
    placed = (
        P("grp", "seq", "rep"),
        P("grp", "seq", "rep"),
        P("grp", "seq", "rep"),
        P("grp", "seq", "rep"),
        P("grp", "seq", "rep"),
        P("grp"),
        P(("grp", "rep"), None, "seq"),
        P(("grp", "rep"), "seq", None, None),
        P(("grp", "rep"), "seq", None, None),
        P(("grp", "rep")),
        P(("grp", "rep")),
        P(("grp", "rep"), None, None),
        P(("grp", "rep"), None, None),
    )
    return jax.shard_map(
        local,
        mesh=mesh,
        in_specs=placed,
        out_specs=(P("grp", "seq", "rep"), P(("grp", "rep"), None, "seq")),
        check_vma=False,
    )
```

time: 321 us -> 104 us (0.32)
  matrix products: 124 us -> 0 us
  Pallas kernels: 0 us -> 96.3 us
  other arithmetic: 56.1 us -> 0.97 us
  blocking collectives: 41.5 us -> 0 us
  starting transfers between devices: 27.5 us -> 0 us
  loops' own time: 24 us -> 0 us
  waiting for transfers between devices: 14.7 us -> 0 us
  between operations: 14.5 us -> 1.31 us
  local copies, waits for them, and re-layouts: 17.1 us -> 5.62 us
    dot_general x32 -> x0, matrix products: 124 us -> none  [the longest x16 73.1 us: online_update(): jnp.einsum(form, weights.astype(jnp.bfloat16), value_rows, preferred_elem...]
    pallas_call x0 -> x1, Pallas kernels: none -> 96.3 us  [local(): pl.pallas_call(kernel, out_shape=(jax.ShapeDtypeStruct((256, 1024), BF16)...]
    all_gather x2 -> x0, blocking collectives: 41.5 us -> none  [the longest x1 21.7 us: local(): lax.all_gather(document_key[0], 'rep', axis=1, tiled=True)]
    another operation x1 -> x0, loops' own time: 24 us -> none  [local(): top, total, summed = lax.scan(one_block, start_state, offsets)[0]]
    all_to_all x2 -> x0, starting transfers between devices: 22.5 us -> none  [the longest x1 11.6 us: local(): lax.all_to_all(run_key, 'seq', split_axis=1, concat_axis=0, tiled=True)]
    reduce_sum x15 -> x0, other arithmetic: 17.6 us -> none  [online_update(): total = total * factor + jnp.sum(weights, axis=-1)]
    lt x13 -> x0, other arithmetic: 15.8 us -> none  [the longest x12 15.7 us: one_block(): hist_ok = shard * hist_rows + within < start_slot]
    ppermute x6 -> x0, waiting for transfers between devices: 8.57 us -> none  [partner(): lax.ppermute(x, axis, [(i, i ^ 1 << stride) for i in range(lax.axis_size(...]
  transfers between devices with their start and end apart: 10 -> 0, of which waited for: 3 -> 0; matrix products, arithmetic and copies ran while one was open for 14% -> 0% of each run, Pallas kernels for 0% -> 0%
where the time goes in v1:
time: 104 us
  Pallas kernels  96.3 us (93%)
  local copies, waits for them, and re-layouts  5.62 us (5%)
  between operations  1.31 us (1%)
    pallas_call x1, Pallas kernels, local(): pl.pallas_call(kernel, out_shape=(jax.ShapeDtypeStruct((256, 1024), BF16)...  96.3 us

profile of v1, /device:TPU:1, one launch (start us, length us, event | category | flops | bytes accessed | tf_op | source)
XLA Modules:
  0.0 104.2 jit_solution(17692407531179849544)
XLA Ops:
  1.3 1.4 %constant_dynamic-slice_fusion = (bf16[32,4,128]{2,1,0:T(4,128)(2,1)}, bf16[32,4,128]{2,1,0:T(4,128)(2,1)}) fusion(bf16[32,4,1024]{2,1,0:T(4,128)(2,1)} %param.25, s32[]{:T(128)S(6)} %select_n.10, bf16[32,4,1024]{2,1,0:T(4,128)(2,1)} %param.24), kind=kLoop, calls=%fused_computation.1 | loop fusion | bytes 131076 | tf_op jit(solution)/shard_map/dynamic_slice | solution.py:432
  2.7 1.0 multiply_convert_fusion
  3.7 0.7 convert_element_type.14.dec_query
  4.4 96.3 %attention.1 = (bf16[256,1024]{1,0:T(8,128)(2,1)}, bf16[512,128]{1,0:T(8,128)(2,1)}) custom-call(bf16[256,1024]{1,0:T(8,128)(2,1)} %bitcast.12, bf16[128,128]{1,0:T(8,128)(2,1)} %bitcast.18, bf16[128,128]{1,0:T(8,128)(2,1)} %bitcast.19, bf16[256,128]{1,0:T(8,128)(2,1)} %bitcast.16, bf16[256,128]{1,0:T(8,128)(2,1)} %bitcast.17, s32[1]{0:T(128)S(6)} %copy.16.start_ref, ...), custom_call_target="tpu_custom_call" | custom-call | tf_op jit(solution)/shard_map/attention/pallas_call | solution.py:439
  100.7 1.6 %reshape.30 = bf16[32,4,512]{2,1,0:T(4,128)(2,1)} reshape(bf16[512,128]{1,0:T(8,128)(2,1)} %get-tuple-element.5) | data formatting | bytes 262144 | tf_op jit(solution)/shard_map/reshape | solution.py:508
  102.4 1.9 %copy.17 = bf16[1,256,1024]{2,1,0:T(8,128)(2,1)} copy(bf16[1,256,1024]{2,1,0:T(8,128)(2,1)} %bitcast.13) | data formatting | bytes 1048576

commit v2 on v1

--- a/solution.py
+++ b/solution.py
@@ -53,13 +53,16 @@
     l_sib,
     dq,
     od_snd,
-    ld_snd,
     od,
-    ld,
+    oc,
+    of,
+    lt,
+    qa,
     dec_o,
-    s0,
     s1,
     s2,
+    d1,
+    d2,
     acc,
     tot,
     mrun,
@@ -73,7 +76,14 @@
     send_sem,
     r0,
     r1,
+    r2,
+    r3,
     rx,
+    ra,
+    rq,
+    ro,
+    rf,
+    own_sem,
 ):
     grp = lax.axis_index("grp")
     seq = lax.axis_index("seq")
@@ -89,14 +99,16 @@
     down = {"seq": seq_at(3, 0)}
     across = {"seq": seq_at(0, 1)}
     sib = {"seq": seq + 1 - 2 * core}
-    doc_seq = ((rep + 1) % 8) * 2 + grp
-    doc_dev = [{"grp": g, "seq": doc_seq, "rep": chip} for g in range(2)]
-    src_rep = (chip + 7) % 8
-    src_dev = [{"grp": core, "seq": 2 * rep + i, "rep": src_rep} for i in range(2)]
+    own_slot = grp * 8 + rep
+    plane = [((chip + k) % 8, {"seq": (chip + k) % 8 * 2 + core}) for k in range(8)]
+    column = []
+    for k in range(16):
+        slot = (own_slot + k) % 16
+        column.append((slot, {"grp": slot // 8, "rep": slot % 8}))
 
     loads = [
-        pltpu.make_async_copy(hist_key, buf.at[seq, pl.ds(0, 128)], in_sem.at[0]),
-        pltpu.make_async_copy(doc_key, buf.at[seq, pl.ds(128, 256)], in_sem.at[1]),
+        pltpu.make_async_copy(hist_key, buf.at[seq, pl.ds(512, 128)], in_sem.at[0]),
+        pltpu.make_async_copy(doc_key, buf.at[seq, pl.ds(0, 256)], in_sem.at[1]),
         pltpu.make_async_copy(hist_value, vals.at[pl.ds(0, 128)], in_sem.at[2]),
         pltpu.make_async_copy(doc_value, vals.at[pl.ds(128, 256)], in_sem.at[3]),
         pltpu.make_async_copy(dec_query, q_own, in_sem.at[4]),
@@ -110,15 +122,15 @@
         c.start()
 
     barrier = pltpu.get_barrier_semaphore()
-    partners = [up, down, across, sib] + doc_dev + src_dev
+    partners = [sib] + [p[1] for p in plane[1:]] + [p[1] for p in column[1:]]
     for d in partners:
         pl.semaphore_signal(barrier, inc=1, device_id=d, device_id_type=MESH)
 
     for c in loads[:4]:
         c.wait()
-    for i in range(3):
+    for i, at in ((0, 640), (1, 256), (2, 384)):
         v = vals[i * 128 : (i + 1) * 128, :]
-        buf[seq, 384 + i * 128 : 512 + i * 128, :] = v.astype(F32).T.astype(BF16)
+        buf[seq, at : at + 128, :] = v.astype(F32).T.astype(BF16)
     loads[4].wait()
     pl.semaphore_wait(barrier, len(partners))
 
@@ -146,36 +158,67 @@
             device_id_type=MESH,
         ).wait_recv()
 
-    first, second = pl.ds(0, 384), pl.ds(384, 384)
-
-    def send_block(b, dev):
-        send(buf.at[b], buf.at[b], r0.at[b], dev)
-
-    def send_first(b, dev):
-        send(buf.at[b, first], buf.at[b, first], r0.at[b], dev)
-
-    def send_second(b, dev):
-        send(buf.at[b, second], buf.at[b, second], r1.at[b], dev)
-
-    def block_in(b):
-        arrived(buf.at[b], r0.at[b])
-
-    def halves_in(b):
-        arrived(buf.at[b, first], r0.at[b])
-        arrived(buf.at[b, second], r1.at[b])
+    class Part:
+        def __init__(self, at, size, sem_a, sem_b):
+            self.whole = pl.ds(at, size)
+            self.first = pl.ds(at, size // 2)
+            self.second = pl.ds(at + size // 2, size // 2)
+            self.sem_a, self.sem_b = sem_a, sem_b
+
+        def send(self, b, *devs):
+            for dev in devs:
+                ref = buf.at[b, self.whole]
+                send(ref, ref, self.sem_a.at[b], dev)
+
+        def send_first(self, b, *devs):
+            for dev in devs:
+                ref = buf.at[b, self.first]
+                send(ref, ref, self.sem_a.at[b], dev)
+
+        def send_second(self, b, *devs):
+            for dev in devs:
+                ref = buf.at[b, self.second]
+                send(ref, ref, self.sem_b.at[b], dev)
+
+        def wait(self, b):
+            arrived(buf.at[b, self.whole], self.sem_a.at[b])
+
+        def wait_first(self, b):
+            arrived(buf.at[b, self.first], self.sem_a.at[b])
+
+        def wait_second(self, b):
+            arrived(buf.at[b, self.second], self.sem_b.at[b])
+
+        def wait_sib(self, row):
+            for x in range(2):
+                self.wait(row * 4 + x * 2 + 1 - core)
+
+    doc = Part(0, 512, r0, r1)
+    hist = Part(512, 256, r2, r3)
+    far, below, above = seq_at(0, 1), seq_at(3, 0), seq_at(1, 0)
+    far_below, far_above = seq_at(3, 1), seq_at(1, 1)
 
     send(q_own, q_sib, rx.at[0], sib)
-    send_block(seq, across)
-    send_block(seq, up)
-    send_block(seq, down)
-    send_block(seq, sib)
-    for g in range(2):
-        send(q_own, dq.at[pl.ds(run * 512, 512)], rx.at[1 + run], doc_dev[g])
-
-    def cache_rows(group, _):
-        for i in range(4):
-            r = group * 4 + i
-            rows = pl.ds(pl.multiple_of(r * 16, 16), 16)
+    doc.send_first(seq, across)
+    doc.send_second(seq, across)
+    doc.send(seq, up, down, sib)
+
+    def piece(ref, i):
+        return ref.at[pl.ds(pl.multiple_of(i * 64, 64), 64)]
+
+    own_copies = [
+        pltpu.make_async_copy(piece(q_own, chip), qa.at[chip], own_sem.at[0]),
+        pltpu.make_async_copy(qa.at[rep], piece(dq, own_slot), own_sem.at[1]),
+        pltpu.make_async_copy(od_snd.at[own_slot], od.at[own_slot], own_sem.at[2]),
+    ]
+    own_copies[0].start()
+    for j, dev in plane[1:]:
+        send(piece(q_own, j), qa.at[chip], ra.at[chip], dev)
+
+    def cache_rows(group):
+        for i in range(8):
+            r = group * 8 + i
+            rows = pl.ds(r * 16, 16)
             q = jnp.concatenate([q_own[rows, :], q_sib[rows, :]], axis=0)
             s = lax.dot_general(q, ck[r], NT, preferred_element_type=F32)
             at = run * 256 + lax.broadcasted_iota(jnp.int32, (32, 256), 1)
@@ -193,27 +236,58 @@
             l_own[rows, :] = top[:16]
             o_snd[rows, :] = o[16:].astype(BF16)
             l_snd[rows, :] = top[16:]
-        return 0
 
     arrived(q_sib, rx.at[0])
     loads[5].wait()
     loads[6].wait()
-    lax.fori_loop(0, 4, cache_rows, 0)
-
-    block_in(seq_at(0, 1))
-    send_block(seq_at(0, 1), up)
-    send_block(seq_at(0, 1), down)
-    send_block(seq_at(0, 1), sib)
-    block_in(seq_at(3, 0))
-    send_first(seq_at(3, 0), up)
-    send_block(seq_at(3, 0), sib)
-    block_in(seq_at(1, 0))
-    send_second(seq_at(1, 0), down)
-    send_block(seq_at(1, 0), sib)
-
-    lax.fori_loop(4, 8, cache_rows, 0)
+    cache_rows(0)
+
+    doc.wait_first(far)
+    doc.send_first(far, up, down)
+    doc.wait(below)
+    doc.send_first(below, up)
+    doc.send(below, sib)
+    doc.wait(above)
+    doc.send_second(above, down)
+    doc.send(above, sib)
+    cache_rows(1)
+    doc.wait_second(far)
+    doc.send_second(far, up, down)
+    doc.send(far, sib)
+    hist.send_first(seq, across)
+    hist.send_second(seq, across)
+    hist.send(seq, up, down, sib)
+
+    own_copies[0].wait()
+    for j, _ in plane[1:]:
+        arrived(qa.at[j], ra.at[j])
+    own_copies[1].start()
+    for slot, dev in column[1:]:
+        send(qa.at[slot % 8], piece(dq, own_slot), rq.at[own_slot], dev)
+    cache_rows(2)
+    doc.wait_first(far_below)
+    doc.send_first(far_below, up)
+    doc.wait_second(far_above)
+    doc.send_second(far_above, down)
+    cache_rows(3)
     send(o_snd, o_sib, rx.at[3], sib)
     send(l_snd, l_sib, rx.at[4], sib)
+
+    doc.wait_second(far_below)
+    doc.send(far_below, sib)
+    doc.wait_first(far_above)
+    doc.send(far_above, sib)
+    hist.wait_first(far)
+    hist.send_first(far, up, down)
+    hist.wait(below)
+    hist.send_first(below, up)
+    hist.send(below, sib)
+    hist.wait(above)
+    hist.send_second(above, down)
+    hist.send(above, sib)
+    hist.wait_second(far)
+    hist.send_second(far, up, down)
+    hist.send(far, sib)
 
     loads[7].wait()
     for h in range(8):
@@ -226,16 +300,16 @@
     macc[...] = jnp.full_like(macc, LOW)
 
     def hist_keys(row):
-        return jnp.concatenate([buf[row * 4 + c, 0:128, :] for c in range(4)], axis=0)
+        return jnp.concatenate([buf[row * 4 + c, 512:640, :] for c in range(4)], axis=0)
 
     def hist_vals(row):
-        return jnp.concatenate([buf[row * 4 + c, 384:512, :] for c in range(4)], axis=1)
+        return jnp.concatenate([buf[row * 4 + c, 640:768, :] for c in range(4)], axis=1)
 
     def doc_keys(c):
-        return jnp.concatenate([buf[c * 2 + i, 128:384, :] for i in range(2)], axis=0)
+        return jnp.concatenate([buf[c * 2 + i, 0:256, :] for i in range(2)], axis=0)
 
     def doc_vals(c):
-        parts = [buf[c * 2 + i, 512 + 128 * j : 640 + 128 * j, :] for i in range(2) for j in range(2)]
+        parts = [buf[c * 2 + i, 256 + 128 * j : 384 + 128 * j, :] for i in range(2) for j in range(2)]
         return jnp.concatenate(parts, axis=1)
 
     def score(q, keys, out, top, mask=None):
@@ -280,88 +354,123 @@
         weigh(s, vals_t, m, pre_state)
         mrun[...] = new
 
-    block_in(seq + 1 - 2 * core)
-    mrun[...] = score(pre_q, doc_keys(chip), s1, mrun[...], causal_mask)
-    block_in(((y * 4) + (1 - xh) * 2) + 1 - core)
+    doc.wait_sib(y)
 
     @pl.when(xh == 1)
     def _():
+        mrun[...] = score(pre_q, doc_keys(chip), s1, mrun[...], causal_mask)
         step(doc_keys(y * 2), s2, None, s1, doc_vals(chip))
-        step(hist_keys(y), s0, hist_mask(y), s2, doc_vals(y * 2))
 
     @pl.when(xh == 0)
     def _():
-        step(hist_keys(y), s0, hist_mask(y), s1, doc_vals(chip))
-
-    block_in(seq_at(3, 1))
-    send_first(seq_at(3, 1), up)
-    send_block(seq_at(3, 1), sib)
-    block_in(seq_at(1, 1))
-    send_second(seq_at(1, 1), down)
-    send_block(seq_at(1, 1), sib)
-
-    def other_in(row):
-        for x in range(2):
-            block_in(row * 4 + x * 2 + 1 - core)
-
-    def row_step(row, last):
+        mrun[...] = score(pre_q, doc_keys(chip), s2, mrun[...], causal_mask)
+
+    for x in range(2):
+        b = seq_at(2, x)
+        doc.wait_first(b)
+        doc.wait_second(b)
+        doc.send(b, sib)
+    hist.wait_first(far_below)
+    hist.send_first(far_below, up)
+    hist.wait_second(far_above)
+    hist.send_second(far_above, down)
+    hist.wait_second(far_below)
+    hist.send(far_below, sib)
+    hist.wait_first(far_above)
+    hist.send(far_above, sib)
+
+    def row_of(k):
+        return (y + jnp.where(k == 0, 0, jnp.where(k == 1, 3, k - 1))) % 4
+
+    def row_step(k, waiting):
+        row = row_of(k)
+        doc.wait_sib(row)
+
         @pl.when(row < y)
         def _():
-            step(doc_keys(row * 2), s1, None, s0, hist_vals(last))
+            step(doc_keys(row * 2), s1, None, s2, doc_vals(waiting))
             step(doc_keys(row * 2 + 1), s2, None, s1, doc_vals(row * 2))
-            step(hist_keys(row), s0, hist_mask(row), s2, doc_vals(row * 2 + 1))
-
-        @pl.when(row > y)
-        def _():
-            weigh(s0, hist_vals(last), mrun[...], pre_state)
-            mrun[...] = score(pre_q, hist_keys(row), s0, mrun[...], hist_mask(row))
-
-    def row_of(k):
-        return (y + jnp.where(k == 0, 0, jnp.where(k == 1, 3, k - 1))) % 4
-
-    def near_row(k, _):
-        row = row_of(k)
-        other_in(row)
-        row_step(row, row_of(k - 1))
-        return 0
-
-    lax.fori_loop(1, 3, near_row, 0)
-
+
+        return jnp.where(row < y, row * 2 + 1, waiting)
+
+    waiting = lax.fori_loop(1, 3, row_step, y * 2)
     for x in range(2):
-        halves_in(seq_at(2, x))
-        send_block(seq_at(2, x), sib)
-    other_in((y + 2) % 4)
-
-    for i in range(2):
-        arrived(dq.at[pl.ds(i * 512, 512)], rx.at[1 + i])
+        b = seq_at(2, x)
+        hist.wait_first(b)
+        hist.wait_second(b)
+        hist.send(b, sib)
+    row = (y + 2) % 4
+    doc.wait_sib(row)
+
+    own_copies[1].wait()
+    for slot, _ in column[1:]:
+        arrived(piece(dq, slot), rq.at[slot])
     dec_state = (dacc, dtot, dmacc)
     dacc[...] = jnp.zeros_like(dacc)
     dtot[...] = jnp.zeros_like(dtot)
     dmacc[...] = jnp.full_like(dmacc, LOW)
-    dmrun[...] = score(dq, doc_keys(0), s1, jnp.full(dmrun.shape, LOW, F32))
+    dmrun[...] = score(dq, doc_keys(0), d1, jnp.full(dmrun.shape, LOW, F32))
 
     def doc_pair(j, _):
         m = dmrun[...]
-        new = score(dq, doc_keys(2 * j + 1), s2, m)
-        weigh(s1, doc_vals(2 * j), m, dec_state)
-        last = score(dq, doc_keys((2 * j + 2) % 8), s1, new)
-        weigh(s2, doc_vals(2 * j + 1), new, dec_state)
+        new = score(dq, doc_keys(2 * j + 1), d2, m)
+        weigh(d1, doc_vals(2 * j), m, dec_state)
+        last = score(dq, doc_keys((2 * j + 2) % 8), d1, new)
+        weigh(d2, doc_vals(2 * j + 1), new, dec_state)
         dmrun[...] = last
         return 0
 
     lax.fori_loop(0, 4, doc_pair, 0)
     total = jnp.sum(dtot[...], axis=0, keepdims=True)
     level = jnp.max(dmacc[...], axis=0, keepdims=True) + jnp.log(total) * LOG2E
-    level = jnp.broadcast_to(level, (8, 1024))
-    for i in range(2):
-        ld_snd[i] = level[:, i * 512 : (i + 1) * 512]
-    od_snd[...] = (dacc[...] / total).T.astype(BF16)
-    for i in range(2):
-        send(od_snd.at[pl.ds(i * 512, 512)], od.at[grp], rx.at[5 + grp], src_dev[i])
-        send(ld_snd.at[i], ld.at[grp], rx.at[7 + grp], src_dev[i])
-
-    row_step((y + 2) % 4, (y + 1) % 4)
-    weigh(s0, hist_vals((y + 2) % 4), mrun[...], pre_state)
+    od_snd[:, 0:64, :] = (dacc[...] / total).T.astype(BF16).reshape(16, 64, 128)
+    line = lax.broadcasted_iota(jnp.int32, (16, 128), 0)
+    for k in range(8):
+        whole = level[:, k * 128 : (k + 1) * 128]
+        high = whole.astype(BF16).astype(F32)
+        mid = (whole - high).astype(BF16).astype(F32)
+        low = whole - high - mid
+        three = jnp.where(line == 0, high, jnp.where(line == 1, mid, jnp.where(line == 2, low, 0.0)))
+        for i in range(2):
+            od_snd[2 * k + i, 64:80, :] = three.astype(BF16)
+    own_copies[2].start()
+    for slot, dev in column[1:]:
+        send(od_snd.at[slot], od.at[own_slot], ro.at[own_slot], dev)
+
+    @pl.when(row < y)
+    def _():
+        step(doc_keys(row * 2), s1, None, s2, doc_vals(waiting))
+        step(doc_keys(row * 2 + 1), s2, None, s1, doc_vals(row * 2))
+
+    waiting = jnp.where(row < y, row * 2 + 1, waiting)
+
+    def hist_pair(a, b, vals_t):
+        hist.wait_sib(a)
+        hist.wait_sib(b)
+        step(hist_keys(a), s1, hist_mask(a), s2, vals_t)
+        step(hist_keys(b), s2, hist_mask(b), s1, hist_vals(a))
+
+    hist_pair(y, (y + 3) % 4, doc_vals(waiting))
+
+    own_copies[2].wait()
+    for slot, _ in column[1:]:
+        arrived(od.at[slot], ro.at[slot])
+    owners = [owner_ref[chip * 4 + i] for i in range(4)]
+    rows_owner = jnp.concatenate([jnp.full((16, 128), o, jnp.int32) for o in owners], axis=0)
+    lane = (lax.broadcasted_iota(jnp.int32, (16, 128), 1) >> 4) & 3
+    lane_owner = jnp.where(
+        lane == 0, owners[0], jnp.where(lane == 1, owners[1], jnp.where(lane == 2, owners[2], owners[3]))
+    )
+    which = jnp.concatenate([rows_owner, lane_owner], axis=0) == 0
+    for h in range(8):
+        chosen = jnp.where(which, od[h].astype(F32), od[8 + h].astype(F32))
+        oc[h] = chosen.astype(BF16)
+    of[chip] = oc[chip]
+    for h, dev in plane[1:]:
+        send(oc.at[h], of.at[chip], rf.at[chip], dev)
+
+    hist_pair((y + 1) % 4, row, hist_vals((y + 3) % 4))
+    weigh(s2, hist_vals(row), mrun[...], pre_state)
     total = jnp.sum(tot[...], axis=0, keepdims=True)
     for h in range(8):
         cols = slice(h * 256, (h + 1) * 256)
@@ -374,18 +483,17 @@
     loads[9].wait()
     arrived(o_sib, rx.at[3])
     arrived(l_sib, rx.at[4])
-    for g in range(2):
-        arrived(od.at[g], rx.at[5 + g])
-        arrived(ld.at[g], rx.at[7 + g])
+    for j, _ in plane[1:]:
+        arrived(of.at[j], rf.at[j])
+    sums = [jnp.sum(of[j, 64:80, :].astype(F32), axis=0, keepdims=True) for j in range(8)]
+    lt[...] = jnp.concatenate(sums * 16, axis=0).T
+    levels = lt[pl.ds(pl.multiple_of(rep % 2 * 64, 64), 64), :]
     for c in range(4):
         rows = slice(c * 128, (c + 1) * 128)
-        own_doc = jnp.concatenate(
-            [jnp.full((16, 128), owner_ref[c * 8 + i], jnp.int32) for i in range(8)], axis=0
+        l_doc = jnp.concatenate(
+            [jnp.broadcast_to(levels[:, j : j + 1], (64, 128)) for j in (2 * c, 2 * c + 1)], axis=0
         )
-        is_first = own_doc == 0
-        levels = [jnp.broadcast_to(ld[g, 0:1, rows], (128, 128)).T for g in range(2)]
-        l_doc = jnp.where(is_first, levels[0], levels[1])
-        o_doc = jnp.where(is_first, od[0, rows, :].astype(F32), od[1, rows, :].astype(F32))
+        o_doc = jnp.concatenate([of[j, 0:64, :].astype(F32) for j in (2 * c, 2 * c + 1)], axis=0)
         s = lax.dot_general(q_own[rows, :], kn[...], NT, preferred_element_type=F32)
         line = c * 128 + lax.broadcasted_iota(jnp.int32, (128, 128), 0)
         col = lax.broadcasted_iota(jnp.int32, (128, 128), 1)
@@ -463,14 +571,17 @@
             vm((512, 128), BF16),
             vm((512, 128), F32),
             vm((1024, 128), BF16),
-            vm((1024, 128), BF16),
-            vm((2, 8, 512), F32),
-            vm((2, 512, 128), BF16),
-            vm((2, 8, 512), F32),
+            vm((16, 80, 128), BF16),
+            vm((16, 80, 128), BF16),
+            vm((8, 80, 128), BF16),
+            vm((8, 80, 128), BF16),
+            vm((128, 128), F32),
+            vm((8, 64, 128), BF16),
             vm((512, 128), BF16),
             vm((512, 2048), F32),
             vm((512, 2048), F32),
-            vm((512, 2048), F32),
+            vm((512, 1024), F32),
+            vm((512, 1024), F32),
             vm((128, 2048), F32),
             vm((8, 2048), F32),
             vm((8, 2048), F32),
@@ -481,10 +592,17 @@
             vm((8, 1024), F32),
             pltpu.SemaphoreType.DMA((10,)),
             pltpu.SemaphoreType.DMA((2,)),
-            pltpu.SemaphoreType.DMA((32,)),
+            pltpu.SemaphoreType.DMA((96,)),
+            pltpu.SemaphoreType.DMA((16,)),
+            pltpu.SemaphoreType.DMA((16,)),
             pltpu.SemaphoreType.DMA((16,)),
             pltpu.SemaphoreType.DMA((16,)),
             pltpu.SemaphoreType.DMA((9,)),
+            pltpu.SemaphoreType.DMA((8,)),
+            pltpu.SemaphoreType.DMA((16,)),
+            pltpu.SemaphoreType.DMA((16,)),
+            pltpu.SemaphoreType.DMA((8,)),
+            pltpu.SemaphoreType.DMA((3,)),
         ],
         compiler_params=pltpu.CompilerParams(
             collective_id=0, has_side_effects=True, vmem_limit_bytes=56 * 1024 * 1024

time: 104 us -> 63.1 us (0.61)
  Pallas kernels: 96.3 us -> 54.4 us
    pallas_call x1, Pallas kernels: 96.3 us -> 54.4 us  [local(): pl.pallas_call(kernel, out_shape=(jax.ShapeDtypeStruct((256, 1024), BF16)...]
where the time goes in v2:
time: 63.1 us; the launch traced here: 62.3 us
  Pallas kernels  54.4 us (86%)
  local copies, waits for them, and re-layouts  5.62 us (9%)
  between operations  1.31 us (2%)
  other arithmetic  0.97 us (2%)
    pallas_call x1, Pallas kernels, local(): pl.pallas_call(kernel, out_shape=(jax.ShapeDtypeStruct((256, 1024), BF16)...  54.4 us
    unnamed x1, local copies, waits for them, and re-layouts  1.87 us
    reshape x1, local copies, waits for them, and re-layouts, local(): return (pre[None], dec.reshape(32, 4, 512))  1.62 us
    dynamic_slice x1, local copies, waits for them, and re-layouts, local(): lax.dynamic_slice_in_dim(decode_value, at, HEAD, 2).reshape(128, HEAD)  1.42 us

profile of v2, /device:TPU:1, one launch (start us, length us, event | category | flops | bytes accessed | tf_op | source)
XLA Modules:
  0.0 62.3 jit_solution(3971937037895657838)
XLA Ops:
  1.3 1.4 %constant_dynamic-slice_fusion = (bf16[32,4,128]{2,1,0:T(4,128)(2,1)}, bf16[32,4,128]{2,1,0:T(4,128)(2,1)}) fusion(bf16[32,4,1024]{2,1,0:T(4,128)(2,1)} %param.25, s32[]{:T(128)S(6)} %select_n.10, bf16[32,4,1024]{2,1,0:T(4,128)(2,1)} %param.24), kind=kLoop, calls=%fused_computation.1 | loop fusion | bytes 131076 | tf_op jit(solution)/shard_map/dynamic_slice | solution.py:540
  2.7 1.0 %multiply_convert_fusion = bf16[32,4,512]{2,1,0:T(4,128)(2,1)S(1)} fusion(bf16[32,4,512]{2,1,0:T(4,128)(2,1)} %param.19), kind=kLoop, calls=%fused_computation | loop fusion | flops 196608 | bytes 262144 | tf_op jit(solution)/shard_map/convert_element_type | solution.py:536
  3.7 0.7 %convert_element_type.14.dec_query = bf16[512,128]{1,0:T(8,128)(2,1)} reshape(bf16[32,4,512]{2,1,0:T(4,128)(2,1)S(1)} %multiply_convert_fusion) | data formatting | bytes 262144 | tf_op jit(solution)/shard_map/convert_element_type | solution.py:536
  4.4 54.4 %attention.1 = (bf16[256,1024]{1,0:T(8,128)(2,1)}, bf16[512,128]{1,0:T(8,128)(2,1)}) custom-call(bf16[256,1024]{1,0:T(8,128)(2,1)} %bitcast.12, bf16[128,128]{1,0:T(8,128)(2,1)} %bitcast.18, bf16[128,128]{1,0:T(8,128)(2,1)} %bitcast.19, bf16[256,128]{1,0:T(8,128)(2,1)} %bitcast.16, bf16[256,128]{1,0:T(8,128)(2,1)} %bitcast.17, s32[1]{0:T(128)S(6)} %copy.16.start_ref, ...), custom_call_target="tpu_custom_call" | custom-call | tf_op jit(solution)/shard_map/attention/pallas_call | solution.py:547
  58.9 1.6 %reshape.30 = bf16[32,4,512]{2,1,0:T(4,128)(2,1)} reshape(bf16[512,128]{1,0:T(8,128)(2,1)} %get-tuple-element.5) | data formatting | bytes 262144 | tf_op jit(solution)/shard_map/reshape | solution.py:626
  60.5 1.9 %copy.17 = bf16[1,256,1024]{2,1,0:T(8,128)(2,1)} copy(bf16[1,256,1024]{2,1,0:T(8,128)(2,1)} %bitcast.13) | data formatting | bytes 1048576

commit v3 on v2

--- a/solution.py
+++ b/solution.py
@@ -84,6 +84,7 @@
     ro,
     rf,
     own_sem,
+    pass_sem,
 ):
     grp = lax.axis_index("grp")
     seq = lax.axis_index("seq")
@@ -106,6 +107,7 @@
         slot = (own_slot + k) % 16
         column.append((slot, {"grp": slot // 8, "rep": slot % 8}))
 
+    own_head = pl.ds(pl.multiple_of(chip * 128, 128), 128)
     loads = [
         pltpu.make_async_copy(hist_key, buf.at[seq, pl.ds(512, 128)], in_sem.at[0]),
         pltpu.make_async_copy(doc_key, buf.at[seq, pl.ds(0, 256)], in_sem.at[1]),
@@ -115,8 +117,8 @@
         pltpu.make_async_copy(cache_key, ck, in_sem.at[5]),
         pltpu.make_async_copy(cache_value, cv, in_sem.at[6]),
         pltpu.make_async_copy(pre_query, pre_raw, in_sem.at[7]),
-        pltpu.make_async_copy(new_key, kn, in_sem.at[8]),
-        pltpu.make_async_copy(new_value, vn, in_sem.at[9]),
+        pltpu.make_async_copy(new_key.at[:, :, own_head], kn, in_sem.at[8]),
+        pltpu.make_async_copy(new_value.at[:, :, own_head], vn, in_sem.at[9]),
     ]
     for c in loads:
         c.start()
@@ -132,6 +134,7 @@
         v = vals[i * 128 : (i + 1) * 128, :]
         buf[seq, at : at + 128, :] = v.astype(F32).T.astype(BF16)
     loads[4].wait()
+    q_own[...] = (q_own[...].astype(F32) * SCALE).astype(BF16)
     pl.semaphore_wait(barrier, len(partners))
 
     sends = []
@@ -365,42 +368,8 @@
     def _():
         mrun[...] = score(pre_q, doc_keys(chip), s2, mrun[...], causal_mask)
 
-    for x in range(2):
-        b = seq_at(2, x)
-        doc.wait_first(b)
-        doc.wait_second(b)
-        doc.send(b, sib)
-    hist.wait_first(far_below)
-    hist.send_first(far_below, up)
-    hist.wait_second(far_above)
-    hist.send_second(far_above, down)
-    hist.wait_second(far_below)
-    hist.send(far_below, sib)
-    hist.wait_first(far_above)
-    hist.send(far_above, sib)
-
     def row_of(k):
         return (y + jnp.where(k == 0, 0, jnp.where(k == 1, 3, k - 1))) % 4
-
-    def row_step(k, waiting):
-        row = row_of(k)
-        doc.wait_sib(row)
-
-        @pl.when(row < y)
-        def _():
-            step(doc_keys(row * 2), s1, None, s2, doc_vals(waiting))
-            step(doc_keys(row * 2 + 1), s2, None, s1, doc_vals(row * 2))
-
-        return jnp.where(row < y, row * 2 + 1, waiting)
-
-    waiting = lax.fori_loop(1, 3, row_step, y * 2)
-    for x in range(2):
-        b = seq_at(2, x)
-        hist.wait_first(b)
-        hist.wait_second(b)
-        hist.send(b, sib)
-    row = (y + 2) % 4
-    doc.wait_sib(row)
 
     own_copies[1].wait()
     for slot, _ in column[1:]:
@@ -409,18 +378,32 @@
     dacc[...] = jnp.zeros_like(dacc)
     dtot[...] = jnp.zeros_like(dtot)
     dmacc[...] = jnp.full_like(dmacc, LOW)
-    dmrun[...] = score(dq, doc_keys(0), d1, jnp.full(dmrun.shape, LOW, F32))
-
-    def doc_pair(j, _):
+
+    def dec_step(keys, out, s, vals_t):
         m = dmrun[...]
-        new = score(dq, doc_keys(2 * j + 1), d2, m)
-        weigh(d1, doc_vals(2 * j), m, dec_state)
-        last = score(dq, doc_keys((2 * j + 2) % 8), d1, new)
-        weigh(d2, doc_vals(2 * j + 1), new, dec_state)
-        dmrun[...] = last
+        new = score(dq, keys, out, m)
+        weigh(s, vals_t, m, dec_state)
+        dmrun[...] = new
+
+    def dec_row(k, _):
+        row = row_of(k)
+        doc.wait_sib(row)
+        dec_step(doc_keys(row * 2), d1, d2, doc_vals(row_of(k - 1) * 2 + 1))
+        dec_step(doc_keys(row * 2 + 1), d2, d1, doc_vals(row * 2))
         return 0
 
-    lax.fori_loop(0, 4, doc_pair, 0)
+    dmrun[...] = score(dq, doc_keys(y * 2), d1, jnp.full(dmrun.shape, LOW, F32))
+    dec_step(doc_keys(y * 2 + 1), d2, d1, doc_vals(y * 2))
+    dec_row(1, 0)
+    for x in range(2):
+        b = seq_at(2, x)
+        doc.wait_first(b)
+        doc.wait_second(b)
+        doc.send(b, sib)
+    dec_row(2, 0)
+    dec_row(3, 0)
+    row = (y + 2) % 4
+    weigh(d2, doc_vals(row * 2 + 1), dmrun[...], dec_state)
     total = jnp.sum(dtot[...], axis=0, keepdims=True)
     level = jnp.max(dmacc[...], axis=0, keepdims=True) + jnp.log(total) * LOG2E
     od_snd[:, 0:64, :] = (dacc[...] / total).T.astype(BF16).reshape(16, 64, 128)
@@ -437,12 +420,30 @@
     for slot, dev in column[1:]:
         send(od_snd.at[slot], od.at[own_slot], ro.at[own_slot], dev)
 
-    @pl.when(row < y)
-    def _():
-        step(doc_keys(row * 2), s1, None, s2, doc_vals(waiting))
-        step(doc_keys(row * 2 + 1), s2, None, s1, doc_vals(row * 2))
-
-    waiting = jnp.where(row < y, row * 2 + 1, waiting)
+    def row_step(k, waiting):
+        row = row_of(k)
+
+        @pl.when(row < y)
+        def _():
+            step(doc_keys(row * 2), s1, None, s2, doc_vals(waiting))
+            step(doc_keys(row * 2 + 1), s2, None, s1, doc_vals(row * 2))
+
+        return jnp.where(row < y, row * 2 + 1, waiting)
+
+    hist.wait_first(far_below)
+    hist.send_first(far_below, up)
+    hist.wait_second(far_above)
+    hist.send_second(far_above, down)
+    hist.wait_second(far_below)
+    hist.send(far_below, sib)
+    hist.wait_first(far_above)
+    hist.send(far_above, sib)
+    waiting = lax.fori_loop(1, 3, row_step, y * 2)
+    for x in range(2):
+        b = seq_at(2, x)
+        hist.wait_first(b)
+        hist.wait_second(b)
+        hist.send(b, sib)
 
     def hist_pair(a, b, vals_t):
         hist.wait_sib(a)
@@ -450,11 +451,7 @@
         step(hist_keys(a), s1, hist_mask(a), s2, vals_t)
         step(hist_keys(b), s2, hist_mask(b), s1, hist_vals(a))
 
-    hist_pair(y, (y + 3) % 4, doc_vals(waiting))
-
-    own_copies[2].wait()
-    for slot, _ in column[1:]:
-        arrived(od.at[slot], ro.at[slot])
+
     owners = [owner_ref[chip * 4 + i] for i in range(4)]
     rows_owner = jnp.concatenate([jnp.full((16, 128), o, jnp.int32) for o in owners], axis=0)
     lane = (lax.broadcasted_iota(jnp.int32, (16, 128), 1) >> 4) & 3
@@ -462,13 +459,34 @@
         lane == 0, owners[0], jnp.where(lane == 1, owners[1], jnp.where(lane == 2, owners[2], owners[3]))
     )
     which = jnp.concatenate([rows_owner, lane_owner], axis=0) == 0
-    for h in range(8):
+    own_copies[2].wait()
+    passed = []
+    for k in (0, 1, 7, 2, 6, 3, 5, 4):
+        h = (rep + k) % 8
+        for g in range(2):
+            slot = (grp + g) % 2 * 8 + h
+            if k + g > 0:
+                arrived(od.at[slot], ro.at[slot])
         chosen = jnp.where(which, od[h].astype(F32), od[8 + h].astype(F32))
         oc[h] = chosen.astype(BF16)
+        copy = pltpu.make_async_remote_copy(
+            src_ref=oc.at[h],
+            dst_ref=of.at[chip],
+            send_sem=pass_sem.at[k],
+            recv_sem=rf.at[chip],
+            device_id={"seq": h * 2 + core},
+            device_id_type=MESH,
+        )
+        passed.append((h, copy))
+
+        @pl.when(h != chip)
+        def _(copy=copy):
+            copy.start()
+
     of[chip] = oc[chip]
-    for h, dev in plane[1:]:
-        send(oc.at[h], of.at[chip], rf.at[chip], dev)
-
+
+    waiting = row_step(3, waiting)
+    hist_pair(y, (y + 3) % 4, doc_vals(waiting))
     hist_pair((y + 1) % 4, row, hist_vals((y + 3) % 4))
     weigh(s2, hist_vals(row), mrun[...], pre_state)
     total = jnp.sum(tot[...], axis=0, keepdims=True)
@@ -481,6 +499,8 @@
 
     loads[8].wait()
     loads[9].wait()
+    new_k = kn[...].astype(F32).reshape(128, 128).astype(BF16)
+    new_v = vn[...].astype(F32).reshape(128, 128).astype(BF16)
     arrived(o_sib, rx.at[3])
     arrived(l_sib, rx.at[4])
     for j, _ in plane[1:]:
@@ -494,7 +514,7 @@
             [jnp.broadcast_to(levels[:, j : j + 1], (64, 128)) for j in (2 * c, 2 * c + 1)], axis=0
         )
         o_doc = jnp.concatenate([of[j, 0:64, :].astype(F32) for j in (2 * c, 2 * c + 1)], axis=0)
-        s = lax.dot_general(q_own[rows, :], kn[...], NT, preferred_element_type=F32)
+        s = lax.dot_general(q_own[rows, :], new_k, NT, preferred_element_type=F32)
         line = c * 128 + lax.broadcasted_iota(jnp.int32, (128, 128), 0)
         col = lax.broadcasted_iota(jnp.int32, (128, 128), 1)
         seen = ((line >> 4) == (col >> 2)) & ((col & 3) <= ((line >> 2) & 3))
@@ -505,7 +525,7 @@
         w_doc = jnp.exp2(l_doc - top)
         w_own = jnp.exp2(l_own[rows, :] - top)
         w_sib = jnp.exp2(l_sib[rows, :] - top)
-        o = lax.dot_general(p.astype(BF16), vn[...], NN, preferred_element_type=F32)
+        o = lax.dot_general(p.astype(BF16), new_v, NN, preferred_element_type=F32)
         o = o + w_doc * o_doc + w_own * o_own[rows, :] + w_sib * o_sib[rows, :].astype(F32)
         weight = jnp.sum(p, axis=1, keepdims=True) + w_doc + w_own + w_sib
         dec_o[rows, :] = (o / weight).astype(BF16)
@@ -513,6 +533,12 @@
     dec_copy.start()
     for c in sends:
         c.wait_send()
+    for h, copy in passed:
+
+        @pl.when(h != chip)
+        def _(copy=copy):
+            copy.wait_send()
+
     pre_copy.wait()
     dec_copy.wait()
 
@@ -532,12 +558,7 @@
     decode_key,
     decode_value,
 ):
-    seq = lax.axis_index("seq")
-    scaled = (decode_query.reshape(32, 4, 4, HEAD).astype(F32) * SCALE).astype(BF16)
-    dec_q = scaled.reshape(512, HEAD)
-    at = seq // 2 * HEAD
-    new_key = lax.dynamic_slice_in_dim(decode_key, at, HEAD, 2).reshape(128, HEAD)
-    new_value = lax.dynamic_slice_in_dim(decode_value, at, HEAD, 2).reshape(128, HEAD)
+    dec_q = decode_query.reshape(512, HEAD)
     smem = pl.BlockSpec(memory_space=pltpu.SMEM)
     hbm = pl.BlockSpec(memory_space=pl.ANY)
 
@@ -562,8 +583,8 @@
             vm((512, 128), BF16),
             vm((32, 256, 128), BF16),
             vm((32, 256, 128), BF16),
-            vm((128, 128), BF16),
-            vm((128, 128), BF16),
+            vm((32, 4, 128), BF16),
+            vm((32, 4, 128), BF16),
             vm((512, 128), F32),
             vm((512, 128), F32),
             vm((512, 128), BF16),
@@ -603,6 +624,7 @@
             pltpu.SemaphoreType.DMA((16,)),
             pltpu.SemaphoreType.DMA((8,)),
             pltpu.SemaphoreType.DMA((3,)),
+            pltpu.SemaphoreType.DMA((8,)),
         ],
         compiler_params=pltpu.CompilerParams(
             collective_id=0, has_side_effects=True, vmem_limit_bytes=56 * 1024 * 1024
@@ -620,8 +642,8 @@
         cached_row_values.reshape(32, 256, HEAD),
         cache_lengths,
         doc_owner,
-        new_key,
-        new_value,
+        decode_key,
+        decode_value,
     )
     return pre[None], dec.reshape(32, 4, 512)
 

time: 63.1 us -> 60.4 us (0.957)
  the two profiles are of different devices: /device:TPU:1 before, /device:TPU:18 now
where the time goes in v3:
time: 60.4 us; the launch traced here: 60.2 us
  Pallas kernels  53.8 us (89%)
  local copies, waits for them, and re-layouts  5.1 us (8%)
  between operations  1.29 us (2%)
    pallas_call x1, Pallas kernels, local(): pl.pallas_call(kernel, out_shape=(jax.ShapeDtypeStruct((256, 1024), BF16)...  53.8 us
    unnamed x1, local copies, waits for them, and re-layouts  1.87 us
    reshape x1, local copies, waits for them, and re-layouts, local(): dec_q = decode_query.reshape(512, HEAD)  1.62 us
    reshape x1, local copies, waits for them, and re-layouts, local(): return (pre[None], dec.reshape(32, 4, 512))  1.62 us

profile of v3, /device:TPU:18, one launch (start us, length us, event | category | flops | bytes accessed | tf_op | source)
XLA Modules:
  0.0 60.2 jit_solution(9597108348548320164)
XLA Ops:
  1.3 1.6 %reshape.16.dec_query = bf16[512,128]{1,0:T(8,128)(2,1)} reshape(bf16[32,4,512]{2,1,0:T(4,128)(2,1)} %param.19) | data formatting | bytes 262144 | tf_op jit(solution)/shard_map/reshape | solution.py:561
  2.9 53.8 %attention.1 = (bf16[256,1024]{1,0:T(8,128)(2,1)}, bf16[512,128]{1,0:T(8,128)(2,1)}) custom-call(bf16[256,1024]{1,0:T(8,128)(2,1)} %bitcast.10, bf16[128,128]{1,0:T(8,128)(2,1)} %bitcast.14, bf16[128,128]{1,0:T(8,128)(2,1)} %bitcast.15, bf16[256,128]{1,0:T(8,128)(2,1)} %bitcast.12, bf16[256,128]{1,0:T(8,128)(2,1)} %bitcast.13, s32[1]{0:T(128)S(6)} %copy.16.start_ref, ...), custom_call_target="tpu_custom_call" | custom-call | tf_op jit(solution)/shard_map/attention/pallas_call | solution.py:568
  56.7 1.6 %reshape.19 = bf16[32,4,512]{2,1,0:T(4,128)(2,1)} reshape(bf16[512,128]{1,0:T(8,128)(2,1)} %get-tuple-element.5) | data formatting | bytes 262144 | tf_op jit(solution)/shard_map/reshape | solution.py:648
  58.3 1.9 %copy.17 = bf16[1,256,1024]{2,1,0:T(8,128)(2,1)} copy(bf16[1,256,1024]{2,1,0:T(8,128)(2,1)} %bitcast.11) | data formatting | bytes 1048576

commit v4 on v3

--- a/solution.py
+++ b/solution.py
@@ -214,9 +214,6 @@
         pltpu.make_async_copy(qa.at[rep], piece(dq, own_slot), own_sem.at[1]),
         pltpu.make_async_copy(od_snd.at[own_slot], od.at[own_slot], own_sem.at[2]),
     ]
-    own_copies[0].start()
-    for j, dev in plane[1:]:
-        send(piece(q_own, j), qa.at[chip], ra.at[chip], dev)
 
     def cache_rows(group):
         for i in range(8):
@@ -253,6 +250,9 @@
     doc.wait(above)
     doc.send_second(above, down)
     doc.send(above, sib)
+    own_copies[0].start()
+    for j, dev in plane[1:]:
+        send(piece(q_own, j), qa.at[chip], ra.at[chip], dev)
     cache_rows(1)
     doc.wait_second(far)
     doc.send_second(far, up, down)
@@ -261,17 +261,17 @@
     hist.send_second(seq, across)
     hist.send(seq, up, down, sib)
 
+    cache_rows(2)
+    doc.wait_first(far_below)
+    doc.send_first(far_below, up)
+    doc.wait_second(far_above)
+    doc.send_second(far_above, down)
     own_copies[0].wait()
     for j, _ in plane[1:]:
         arrived(qa.at[j], ra.at[j])
     own_copies[1].start()
     for slot, dev in column[1:]:
         send(qa.at[slot % 8], piece(dq, own_slot), rq.at[own_slot], dev)
-    cache_rows(2)
-    doc.wait_first(far_below)
-    doc.send_first(far_below, up)
-    doc.wait_second(far_above)
-    doc.send_second(far_above, down)
     cache_rows(3)
     send(o_snd, o_sib, rx.at[3], sib)
     send(l_snd, l_sib, rx.at[4], sib)
@@ -280,17 +280,6 @@
     doc.send(far_below, sib)
     doc.wait_first(far_above)
     doc.send(far_above, sib)
-    hist.wait_first(far)
-    hist.send_first(far, up, down)
-    hist.wait(below)
-    hist.send_first(below, up)
-    hist.send(below, sib)
-    hist.wait(above)
-    hist.send_second(above, down)
-    hist.send(above, sib)
-    hist.wait_second(far)
-    hist.send_second(far, up, down)
-    hist.send(far, sib)
 
     loads[7].wait()
     for h in range(8):
@@ -400,6 +389,17 @@
         doc.wait_first(b)
         doc.wait_second(b)
         doc.send(b, sib)
+    hist.wait_first(far)
+    hist.send_first(far, up, down)
+    hist.wait(below)
+    hist.send_first(below, up)
+    hist.send(below, sib)
+    hist.wait(above)
+    hist.send_second(above, down)
+    hist.send(above, sib)
+    hist.wait_second(far)
+    hist.send_second(far, up, down)
+    hist.send(far, sib)
     dec_row(2, 0)
     dec_row(3, 0)
     row = (y + 2) % 4

time: 60.4 us -> 63.9 us (1.058)
  the two profiles are of different devices: /device:TPU:18 before, /device:TPU:22 now
where the time goes in v4:
time: 63.9 us; the launch traced here: 63.8 us
  Pallas kernels  57.4 us (90%)
  local copies, waits for them, and re-layouts  5.1 us (8%)
  between operations  1.29 us (2%)
    pallas_call x1, Pallas kernels, local(): pl.pallas_call(kernel, out_shape=(jax.ShapeDtypeStruct((256, 1024), BF16)...  57.4 us
    unnamed x1, local copies, waits for them, and re-layouts  1.87 us
    reshape x1, local copies, waits for them, and re-layouts, local(): dec_q = decode_query.reshape(512, HEAD)  1.62 us
    reshape x1, local copies, waits for them, and re-layouts, local(): return (pre[None], dec.reshape(32, 4, 512))  1.62 us

profile of v4, /device:TPU:22, one launch (start us, length us, event | category | flops | bytes accessed | tf_op | source)
XLA Modules:
  0.0 63.8 jit_solution(9401591048782421642)
XLA Ops:
  1.3 1.6 %reshape.16.dec_query = bf16[512,128]{1,0:T(8,128)(2,1)} reshape(bf16[32,4,512]{2,1,0:T(4,128)(2,1)} %param.19) | data formatting | bytes 262144 | tf_op jit(solution)/shard_map/reshape | solution.py:561
  2.9 57.4 %attention.1 = (bf16[256,1024]{1,0:T(8,128)(2,1)}, bf16[512,128]{1,0:T(8,128)(2,1)}) custom-call(bf16[256,1024]{1,0:T(8,128)(2,1)} %bitcast.10, bf16[128,128]{1,0:T(8,128)(2,1)} %bitcast.14, bf16[128,128]{1,0:T(8,128)(2,1)} %bitcast.15, bf16[256,128]{1,0:T(8,128)(2,1)} %bitcast.12, bf16[256,128]{1,0:T(8,128)(2,1)} %bitcast.13, s32[1]{0:T(128)S(6)} %copy.16.start_ref, ...), custom_call_target="tpu_custom_call" | custom-call | tf_op jit(solution)/shard_map/attention/pallas_call | solution.py:568
  60.3 1.6 %reshape.19 = bf16[32,4,512]{2,1,0:T(4,128)(2,1)} reshape(bf16[512,128]{1,0:T(8,128)(2,1)} %get-tuple-element.5) | data formatting | bytes 262144 | tf_op jit(solution)/shard_map/reshape | solution.py:648
  61.9 1.9 %copy.17 = bf16[1,256,1024]{2,1,0:T(8,128)(2,1)} copy(bf16[1,256,1024]{2,1,0:T(8,128)(2,1)} %bitcast.11) | data formatting | bytes 1048576
